TPU v7x, 512 devices: a whole 4x4x16 slice. The times are simulated.
512 devices in a mesh: node: 32 (over z, core), feat: 16 (over x, y).
Axes of the slice: x: 4, y: 4, z: 16, core: 2. Of those that a mesh axis runs over, the one named last changes fastest.
Arguments:
- features: bfloat16 [65536, 768], P('node', 'feat'), may hold values from -6 to 6
- weight: bfloat16 [768, 512], P('feat'), may hold values from -0.21875 to 0.21875
- bias: float32 [512], replicated, may hold values from -3 to 3
- tile_src: int32 [512, 32], P(('node', 'feat')), may hold values from 0 to 511, as said below
- tile_count: int32 [512], P(('node', 'feat')), may hold values from 2 to 32, as said below
- tile_vals: bfloat16 [512, 32, 128, 128], P(('node', 'feat')), may hold values from -0.125 to 0.125
Outputs:
- activated: bfloat16 [65536, 512], P(('node', 'feat'))
Inputs may be any that keep to these rules, and one draw needn't show every extreme that they name: Block b of hidden belongs to node partition b // 16. In every row of tile_src the live slots (and all slots) name at most 2 blocks of any one node partition, and one partition supplies exactly 2 live slots in every row. `tile_count`: counts are uneven across destination blocks; some block is full in every draw.
All inputs are finite; a program needn't handle non-finite values.
Results may differ from a plain program's by a relative error of at most 0.0045.
Values may be sent and summed in bfloat16 or wider, within the bound.
A program may use at most 64 MiB of HBM per device.

v0:
```python
import jax
import jax.numpy as jnp
from jax import lax
from jax.sharding import PartitionSpec as P


def shards(features, weight, bias, tile_src, tile_count, tile_vals):
    feat_count = lax.axis_size("feat")
    node_count = lax.axis_size("node")
    block_rows = tile_vals.shape[2]
    tile_total = tile_src.shape[1]
    capacity = max(2, 2 * tile_total // node_count)
    own_rows = lax.all_to_all(features, "feat", split_axis=0, concat_axis=1, tiled=True)
    full_weight = lax.all_gather(weight, "feat", axis=0, tiled=True)
    hidden = jnp.dot(own_rows, full_weight, preferred_element_type=jnp.float32).astype(jnp.bfloat16)
    partition_rows = lax.all_gather(hidden, "feat", axis=0, tiled=True)
    group_blocks = partition_rows.reshape(feat_count, block_rows, hidden.shape[1])
    sources = tile_src[0]
    alive = jnp.arange(tile_total) < tile_count[0]
    owners = sources // feat_count
    inside_index = sources % feat_count
    matches = ((owners[:, None] == jnp.arange(node_count)[None, :]) & alive[:, None]).astype(
        jnp.int32
    )
    earlier = jnp.cumsum(matches, axis=0) - matches
    position = jnp.sum(earlier * matches, axis=1)
    slot_index = jnp.where(alive, owners * capacity + position, 0)
    slot_matches = (
        alive[:, None] & (slot_index[:, None] == jnp.arange(node_count * capacity)[None, :])
    ).astype(jnp.int32)
    requests = jnp.sum(slot_matches * inside_index[:, None], axis=0).reshape(node_count, capacity)
    picked = group_blocks[lax.all_to_all(requests, "node", split_axis=0, concat_axis=0, tiled=True)]
    received = lax.all_to_all(picked, "node", split_axis=0, concat_axis=0, tiled=True)
    flattened = received.reshape(node_count * capacity, block_rows, hidden.shape[1])
    fetched = flattened[slot_index]
    live_vals = jnp.where(alive[:, None, None], tile_vals[0], jnp.zeros((), jnp.bfloat16))
    summed = jnp.einsum("tij,tjh->ih", live_vals, fetched, preferred_element_type=jnp.float32)
    return jax.nn.relu(summed + bias).astype(jnp.bfloat16)


def solution(mesh):
    placed = (
        P("node", "feat"),
        P("feat", None),
        P(),
        P(("node", "feat"), None),
        P(("node", "feat")),
        P(("node", "feat"), None, None, None),
    )
    return jax.shard_map(
        shards, mesh=mesh, in_specs=placed, out_specs=P(("node", "feat"), None), check_vma=False
    )
```

profile of v0, /device:TPU:1, one launch (start us, length us, event | category | flops | bytes accessed | tf_op | source)
XLA Modules:
  0.0 501.9 jit_solution(11742805848851607725)
XLA Ops:
  6.5 0.0 copy-start
  6.5 0.9 copy-done
  7.5 0.7 copy_bitcast_fusion
  8.2 7.6 %all-to-all-start = ((bf16[16,128,48]{1,2,0:T(8,128)(2,1)}), bf16[16,128,48]{1,2,0:T(8,128)(2,1)S(1)}, u32[]{:S(2)}, u32[]{:S(2)}) async-start(bf16[16,128,48]{1,2,0:T(8,128)(2,1)} %copy_bitcast_fusion), calls=%async_computation | async-start | bytes 393216 | tf_op jit(solution)/shard_map/all_to_all | solution.py:13
  15.8 0.0 all-gather.2.cloned.1.call-start
  15.8 20.1 %all_gather.6 = bf16[768,512]{1,0:T(8,128)(2,1)S(1)} all-gather(bf16[48,512]{1,0:T(8,128)(2,1)} %param.7), channel_id=1, replica_groups=mesh['node'=32,'feat'=16] {'feat'}, dimensions={0}, use_global_device_ids=true | all-gather | bytes 835584 | tf_op jit(solution)/shard_map/all_gather | solution.py:14
  35.9 0.0 all-to-all-done
  35.9 0.9 convolution_convert_fusion
  36.9 0.0 all-gather.2.cloned.1.call-update
  37.6 0.7 and_select_fusion.2
  38.2 0.1 fusion.6
  38.3 0.1 reduce_window_sum.11
  38.4 0.2 select_reduce_fusion.1
  38.6 0.1 select_reduce_fusion
  38.7 0.1 all_to_all.29
  38.8 32.4 %all_to_all.36 = s32[32,1,2]{2,1,0:T(1,128)S(1)} all-to-all(s32[32,1,2]{2,1,0:T(1,128)S(1)} %bitcast.72), channel_id=1, replica_groups=mesh['node'=32,'feat'=16] {'node'}, dimensions={0} | all-to-all | bytes 512 | tf_op jit(solution)/shard_map/all_to_all | solution.py:32
  71.2 0.1 copy.20
  71.3 0.1 copy.21
  71.4 0.1 reshape.194
  71.5 32.2 %all-gather.2.cloned.1.call-done = bf16[2048,512]{1,0:T(8,128)(2,1)} async-done(((bf16[128,512]{1,0:T(8,128)(2,1)}), bf16[2048,512]{1,0:T(8,128)(2,1)}) %all-gather.2.cloned.1.call-update) | async-done | bytes 2097168 | tf_op jit(solution)/shard_map/all_gather | solution.py:16
  103.7 6.9 %gather_fusion = bf16[64,128,512]{2,1,0:T(8,128)(2,1)} fusion(bf16[16,128,512]{2,1,0:T(8,128)(2,1)} %bitcast.69, s32[1024]{0:T(1024)S(1)} %pad_clamp_fusion.1), kind=kCustom, calls=%fused_computation | custom fusion | bytes 16777472 | tf_op jit(solution)/shard_map/gather | solution.py:32
  110.6 0.0 copy-start.1
  110.6 14.0 %all-to-all-start.2 = ((bf16[32,2,128,512]{3,2,1,0:T(8,128)(2,1)}), bf16[32,2,128,512]{3,2,1,0:T(8,128)(2,1)}, u32[]{:S(2)}, u32[]{:S(2)}) async-start(bf16[32,2,128,512]{3,2,1,0:T(8,128)(2,1)} %bitcast.70), calls=%async_computation.2 | async-start | bytes 16777216 | tf_op jit(solution)/shard_map/all_to_all | solution.py:33
  124.6 0.0 copy-done.1
  124.6 360.6 %all-to-all-done.2 = bf16[32,2,128,512]{3,2,1,0:T(8,128)(2,1)} async-done(((bf16[32,2,128,512]{3,2,1,0:T(8,128)(2,1)}), bf16[32,2,128,512]{3,2,1,0:T(8,128)(2,1)}, u32[]{:S(2)}, u32[]{:S(2)}) %all-to-all-start.2) | async-done | bytes 8388640 | tf_op jit(solution)/shard_map/all_to_all | solution.py:33
  485.2 0.0 copy-start.2
  485.2 0.0 copy-start.3
  485.2 6.2 %gather_fusion.1 = bf16[32,128,512]{2,1,0:T(8,128)(2,1)} fusion(bf16[64,128,512]{2,1,0:T(8,128)(2,1)} %bitcast.9, s32[1024]{0:T(1024)S(1)} %pad_clamp_fusion), kind=kCustom, calls=%fused_computation.1 | custom fusion | bytes 8388736 | tf_op jit(solution)/shard_map/gather | solution.py:35
  491.4 0.0 copy-done.2
  491.4 0.0 copy-done.3
  491.4 3.6 fusion.2
  (6 shorter events, 0.0 us)
Async XLA Ops:
  6.5 0.9 copy-start
  8.2 27.8 %all-to-all-start = ((bf16[16,128,48]{1,2,0:T(8,128)(2,1)}), bf16[16,128,48]{1,2,0:T(8,128)(2,1)S(1)}, u32[]{:S(2)}, u32[]{:S(2)}) async-start(bf16[16,128,48]{1,2,0:T(8,128)(2,1)} %copy_bitcast_fusion), calls=%async_computation | async-start | bytes 393216 | tf_op jit(solution)/shard_map/all_to_all | solution.py:13
  15.8 87.9 %all-gather.2.cloned.1.call-start = ((), (), s32[]{:S(2)}) async-start(), calls=%async_computation.3 | async-start | bytes 2228224 | tf_op jit(solution)/shard_map/all_gather | solution.py:16
  110.6 14.0 %copy-start.1 = (s32[1,32]{1,0:T(1,128)S(1)}, s32[1,32]{1,0:T(1,128)}, u32[]{:S(2)}) copy-start(s32[1,32]{1,0:T(1,128)} %param.9) | copy-start | bytes 388
  110.6 374.6 %all-to-all-start.2 = ((bf16[32,2,128,512]{3,2,1,0:T(8,128)(2,1)}), bf16[32,2,128,512]{3,2,1,0:T(8,128)(2,1)}, u32[]{:S(2)}, u32[]{:S(2)}) async-start(bf16[32,2,128,512]{3,2,1,0:T(8,128)(2,1)} %bitcast.70), calls=%async_computation.2 | async-start | bytes 16777216 | tf_op jit(solution)/shard_map/all_to_all | solution.py:33
  485.2 6.2 %copy-start.2 = (bf16[1,32,128,128]{3,2,1,0:T(8,128)(2,1)S(1)}, bf16[1,32,128,128]{3,2,1,0:T(8,128)(2,1)}, u32[]{:S(2)}) copy-start(bf16[1,32,128,128]{3,2,1,0:T(8,128)(2,1)} %param.11) | copy-start | bytes 3145732
  485.2 6.2 %copy-start.3 = (f32[512]{0:T(512)S(1)}, f32[512]{0:T(512)}, u32[]{:S(2)}) copy-start(f32[512]{0:T(512)} %param.8) | copy-start | bytes 6148
Sparse Core Ops, SparseCore 0:
  37.0 66.5 all-gather.1
where the time goes:
time: 510 us; the launch traced here: 502 us
  waiting for transfers between devices  393 us (77%)
  blocking collectives  52.5 us (10%)
  starting transfers between devices  21.6 us (4%)
  local copies, waits for them, and re-layouts  15.2 us (3%)
  between operations  14.1 us (3%)
    all_to_all x1, waiting for transfers between devices, shards(): lax.all_to_all(picked, 'node', split_axis=0, concat_axis=0, tiled=True)  361 us
    all_to_all x1, blocking collectives, shards(): lax.all_to_all(requests, 'node', split_axis=0, concat_axis=0, tiled=True)  32.4 us
    all_gather x1, waiting for transfers between devices, shards(): partition_rows = lax.all_gather(hidden, 'feat', axis=0, tiled=True)  32.2 us
    all_gather x1, blocking collectives, shards(): full_weight = lax.all_gather(weight, 'feat', axis=0, tiled=True)  20.1 us
    all_to_all x1, starting transfers between devices, shards(): lax.all_to_all(picked, 'node', split_axis=0, concat_axis=0, tiled=True)  14 us
  transfers between devices with their start and end apart: 3, of which 2 were waited for; matrix products, arithmetic and copies ran while one was open for 0% of the time, Pallas kernels for 0%

commit v1 on v0

v1 whole, which is shorter than its diff:
```python
import jax
import jax.numpy as jnp
from jax import lax
from jax.experimental import pallas as pl
from jax.experimental.pallas import tpu as pltpu
from jax.sharding import PartitionSpec as P

MESH = pl.DeviceIdType.MESH
NX, NY, NZ = 4, 4, 16
BLK = 128
COLS = 64
GROUP = 2 * NX
PART = 5
SHARD = 8
HALF = 3
BLOCKS = NZ * NY * SHARD
SLOTS = 32
UNROLL = 8


def kernel(
    ft, w, bias, src, cnt, tiles, out,
    xbuf, wbuf, hb, stage, tbuf, sv, ss, bt, obuf, rbuf,
    x_sem, w_sem, s_sem, ss_sem, t_sem, local_sem, h_sem, ry_sem, pz_sem, rz_sem, py_sem, pf_sem, o_sem,
):
    n = lax.axis_index("node")
    f = lax.axis_index("feat")
    z, c = lax.div(n, 2), lax.rem(n, 2)
    x, y = lax.div(f, NY), lax.rem(f, NY)
    me = x * 2 + c

    def at(xx, yy, zz, cc):
        return (zz * 2 + cc, xx * NY + yy)

    def up(value, size, by=1):
        return lax.rem(value + by, size)

    def down(value, size, by=1):
        return lax.rem(value + size - by, size)

    def remote(source, target, sems, index, device):
        return pltpu.make_async_remote_copy(
            src_ref=source, dst_ref=target, send_sem=sems.at[(0,) + index], recv_sem=sems.at[(1,) + index],
            device_id=device, device_id_type=MESH,
        )

    sibling = at(x, y, z, 1 - c)
    right, left = at(up(x, NX), y, z, c), at(down(x, NX), y, z, c)
    front, back = at(x, up(y, NY), z, c), at(x, down(y, NY), z, c)
    above, below = at(x, y, up(z, NZ), c), at(x, y, down(z, NZ), c)

    def group_peer(i):
        other = lax.rem(me + i, GROUP)
        return other, at(lax.div(other, 2), y, z, lax.rem(other, 2))

    barrier = pltpu.get_barrier_semaphore()

    @pl.loop(1, NX * NY)
    def _(i):
        pl.semaphore_signal(barrier, inc=1, device_id=(n, lax.rem(f + i, NX * NY)), device_id_type=MESH)

    for i in range(1, NX):
        pl.semaphore_signal(barrier, inc=1, device_id=at(up(x, NX, i), y, z, 1 - c), device_id_type=MESH)
    for device in (sibling, above, below):
        pl.semaphore_signal(barrier, inc=1, device_id=device, device_id_type=MESH)

    s = src[...]
    zz, rest = lax.shift_right_logical(s, 5), s & 31
    cc, ff = lax.shift_right_logical(rest, 4), rest & 15
    place = (zz * NY + lax.shift_right_logical(ff, 2)) * SHARD + cc * 4 + (ff & 3)
    alive = lax.broadcasted_iota(jnp.int32, s.shape, 1) < cnt[0]
    sv[me] = jnp.zeros((8, 128), jnp.int32)
    sv[me, 0:1, 0:SLOTS] = jnp.where(alive, place, BLOCKS)
    hb[BLOCKS] = jnp.zeros((COLS, BLK), jnp.bfloat16)
    bt[...] = jnp.broadcast_to(bias[pl.ds(x, 1), :], (128, 128)).T

    pl.semaphore_wait(barrier, NX * NY - 1 + NX - 1 + 3)

    def x_copy(i):
        peer = lax.rem(f + i, NX * NY)
        return remote(ft.at[lax.rem(peer, NY)], xbuf.at[f], x_sem, (i - 1,), (n, peer))

    def w_copy(i):
        peer = lax.rem(f + i, NX * NY)
        columns = pl.ds(pl.multiple_of(lax.div(peer, NY) * 128, 128), 128)
        return remote(w.at[:, columns], wbuf.at[f], w_sem, (i - 1,), (n, peer))

    @pl.loop(1, NX * NY)
    def _(i):
        x_copy(i).start()
        w_copy(i).start()

    xbuf[f] = ft[y]
    wbuf[f] = w[:, pl.ds(pl.multiple_of(x * 128, 128), 128)]

    def s_copy(i):
        _, device = group_peer(i)
        return remote(sv.at[me], sv.at[me], s_sem, (i - 1,), device)

    for i in range(1, GROUP):
        s_copy(i).start()

    @pl.loop(1, NX * NY)
    def _(i):
        x_copy(i).wait_recv()
        w_copy(i).wait_recv()

    own = tiles.at[0]
    low, high = pl.ds(0, SLOTS // 2), pl.ds(SLOTS // 2, SLOTS // 2)
    keep = pltpu.make_async_copy(own, tbuf.at[me], local_sem.at[0])
    keep.start()
    t_low_right = remote(own.at[low], tbuf.at[me, low], t_sem, (0,), right)
    t_high_left = remote(own.at[high], tbuf.at[me, high], t_sem, (1,), left)
    t_high_right = remote(own.at[high], tbuf.at[me, high], t_sem, (2,), right)
    t_low_left = remote(own.at[low], tbuf.at[me, low], t_sem, (3,), left)
    t_own_sibling = remote(own, tbuf.at[me], t_sem, (4,), sibling)
    for copy in (t_low_right, t_high_left, t_high_right, t_low_left, t_own_sibling):
        copy.start()
    from_left, from_right, from_far = (down(x, NX) * 2 + c, up(x, NX) * 2 + c, up(x, NX, 2) * 2 + c)
    t_pass_right = remote(tbuf.at[from_left, low], tbuf.at[from_left, low], t_sem, (5,), right)
    t_pass_left = remote(tbuf.at[from_right, high], tbuf.at[from_right, high], t_sem, (6,), left)
    t_sibling = [
        remote(tbuf.at[e], tbuf.at[e], t_sem, (7 + j,), sibling)
        for j, e in enumerate((from_left, from_right, from_far))
    ]

    ht = lax.dot_general(
        wbuf[...].reshape(NX * NY * 48, 128), xbuf[...].reshape(NX * NY * 48, 512),
        (((0,), (0,)), ((), ())), preferred_element_type=jnp.float32,
    ).astype(jnp.bfloat16)
    mine = jnp.where(c == 0, ht[:COLS], ht[COLS:])
    other = jnp.where(c == 0, ht[COLS:], ht[:COLS])
    place_of = lambda zz, yy: (zz * NY + yy) * SHARD
    base = place_of(z, y) + c * 4
    for k in range(4):
        stage[k] = other[:, k * BLK : (k + 1) * BLK]
    h_copy = remote(stage, hb.at[pl.ds(base, 4)], h_sem, (0,), sibling)
    h_copy.start()
    for k in range(4):
        hb[base + k] = mine[:, k * BLK : (k + 1) * BLK]
    h_copy.wait_recv()

    def blocks(zz, yy, first, count):
        return hb.at[pl.ds(place_of(zz, yy) + first, count)]

    def ry_copy(j):
        ref = blocks(z, y, PART, SHARD - PART)
        return remote(ref, ref, ry_sem, (j - 1,), at(x, up(y, NY, j), z, c))

    def pz_copy(zz, step, direction, first=0, count=PART):
        ref = blocks(zz, y, first, count)
        return remote(ref, ref, pz_sem, (direction, step), (above, below)[direction])

    hz = hb.at[pl.ds(0, BLOCKS)].reshape(NZ, NY, SHARD, COLS, BLK)

    def rz_copy(zz, step, direction, first=0, count=NY):
        ref = hz.at[zz, pl.ds(first, count), pl.ds(PART, SHARD - PART)]
        return remote(ref, ref, rz_sem, (direction, step), (above, below)[direction])

    def py_copy(zz, yy, direction):
        ref = blocks(zz, yy, 0, PART)
        return remote(ref, ref, py_sem, (direction, zz), (front, back)[direction])

    def pf_copy(zz, yy, direction):
        ref = blocks(zz, yy, *((0, HALF), (HALF, PART - HALF))[direction])
        return remote(ref, ref, pf_sem, (direction, zz), (front, back)[direction])

    far = NZ // 2
    pz_copy(z, 0, 0).start()
    pz_copy(z, 0, 1).start()
    for j in range(1, NY):
        ry_copy(j).start()
    py_copy(z, y, 0).start()
    py_copy(z, y, 1).start()
    for j in range(1, NY):
        ry_copy(j).wait_recv()
    rz_copy(z, 0, 0).start()
    rz_copy(z, 0, 1).start()

    def p_arrived(step):
        lower, upper = down(z, NZ, step), up(z, NZ, step)
        pz_copy(lower, step - 1, 0).wait_recv()
        pz_copy(upper, step - 1, 1).wait_recv()
        return lower, upper

    @pl.loop(1, far - 1)
    def _(step):
        lower, upper = p_arrived(step)
        pz_copy(lower, step, 0).start()
        pz_copy(upper, step, 1).start()
        for zz in (lower, upper):
            py_copy(zz, y, 0).start()
            py_copy(zz, y, 1).start()

    lower, upper = p_arrived(far - 1)
    pz_last = (
        pz_copy(lower, far - 1, 0, 0, HALF),
        pz_copy(upper, far - 1, 1, HALF, PART - HALF),
    )
    for copy in pz_last:
        copy.start()
    for zz in (lower, upper):
        py_copy(zz, y, 0).start()
        py_copy(zz, y, 1).start()
    opposite = up(z, NZ, far)
    pz_copy(opposite, far - 1, 0, 0, HALF).wait_recv()
    pz_copy(opposite, far - 1, 1, HALF, PART - HALF).wait_recv()
    py_copy(opposite, y, 0).start()
    py_copy(opposite, y, 1).start()

    def pass_on(zz):
        py_copy(zz, down(y, NY), 0).wait_recv()
        pf_copy(zz, down(y, NY), 0).start()
        py_copy(zz, up(y, NY), 1).wait_recv()
        pf_copy(zz, up(y, NY), 1).start()

    def r_arrived(step):
        lower, upper = down(z, NZ, step), up(z, NZ, step)
        rz_copy(lower, step - 1, 0).wait_recv()
        rz_copy(upper, step - 1, 1).wait_recv()
        return lower, upper

    def r_step(step):
        lower, upper = r_arrived(step)
        rz_copy(lower, step, 0).start()
        rz_copy(upper, step, 1).start()
        return lower, upper

    pass_on(z)
    pass_on(opposite)

    def both(step):
        lower, upper = r_step(step)
        pass_on(lower)
        pass_on(upper)

    @pl.loop(1, 4)
    def _(step):
        both(step)

    t_low_right.wait_recv()
    t_pass_right.start()
    t_high_left.wait_recv()
    t_pass_left.start()
    t_high_right.wait_recv()
    t_sibling[0].start()
    t_low_left.wait_recv()
    t_sibling[1].start()

    @pl.loop(4, far - 1)
    def _(step):
        both(step)

    lower, upper = r_arrived(far - 1)
    rz_last = (
        rz_copy(lower, far - 1, 0, 0, NY // 2),
        rz_copy(upper, far - 1, 1, NY // 2, NY // 2),
    )
    for copy in rz_last:
        copy.start()
    pass_on(lower)
    pass_on(upper)

    remote(tbuf.at[from_far, low], tbuf.at[from_far, low], t_sem, (5,), right).wait_recv()
    remote(tbuf.at[from_far, high], tbuf.at[from_far, high], t_sem, (6,), left).wait_recv()
    t_sibling[2].start()

    rz_copy(opposite, far - 1, 0, 0, NY // 2).wait_recv()
    rz_copy(opposite, far - 1, 1, NY // 2, NY // 2).wait_recv()

    @pl.loop(0, NZ)
    def _(zz):
        pf_copy(zz, up(y, NY, 2), 0).wait_recv()
        pf_copy(zz, up(y, NY, 2), 1).wait_recv()

    for i in range(1, GROUP):
        s_copy(i).wait_recv()
    places = pltpu.make_async_copy(sv, ss, ss_sem.at[0])
    places.start()
    keep.wait()
    t_own_sibling.wait_recv()
    for copy in t_sibling:
        copy.wait_recv()
    places.wait()

    def aggregate(e):
        total = jnp.zeros((COLS, BLK), jnp.float32)
        for first in range(0, SLOTS, UNROLL):
            slots = range(first, first + UNROLL)
            picked = jnp.concatenate([hb[ss[e, 0, t]] for t in slots], axis=1)
            values = jnp.concatenate([tbuf[e, t] for t in slots], axis=1)
            total += lax.dot_general(
                picked, values, (((1,), (1,)), ((), ())), preferred_element_type=jnp.float32
            )
        return jnp.maximum(total + bt[pl.ds(pl.multiple_of(c * COLS, COLS), COLS), :], 0.0).astype(jnp.bfloat16)

    def o_copy(i):
        _, device = group_peer(i)
        return remote(obuf.at[i], rbuf.at[me], o_sem, (i - 1,), device)

    @pl.loop(1, GROUP)
    def _(i):
        e, _ = group_peer(i)
        obuf[i] = aggregate(e)
        o_copy(i).start()

    rbuf[me] = aggregate(me)

    @pl.loop(1, NX * NY)
    def _(i):
        x_copy(i).wait_send()
        w_copy(i).wait_send()

    for i in range(1, GROUP):
        s_copy(i).wait_send()
    for copy in (t_low_right, t_high_left, t_high_right, t_low_left, t_own_sibling, t_pass_right, t_pass_left, h_copy):
        copy.wait_send()
    for copy in t_sibling + list(pz_last) + list(rz_last):
        copy.wait_send()
    for j in range(1, NY):
        ry_copy(j).wait_send()

    @pl.loop(0, far - 1)
    def _(step):
        for direction in range(2):
            pz_copy(z, step, direction).wait_send()
            rz_copy(z, step, direction).wait_send()

    @pl.loop(0, NZ)
    def _(zz):
        for direction in range(2):
            py_copy(zz, y, direction).wait_send()
            pf_copy(zz, y, direction).wait_send()

    @pl.loop(1, GROUP)
    def _(i):
        o_copy(i).wait_recv()

    out[...] = rbuf[...].reshape(GROUP * COLS, BLK)

    @pl.loop(1, GROUP)
    def _(i):
        o_copy(i).wait_send()


def shards(features, weight, bias, tile_src, tile_count, tile_vals):
    rows, depth = features.shape
    ft = features.reshape(NY, rows // NY, depth).transpose(0, 2, 1)
    vmem = pl.BlockSpec(memory_space=pltpu.VMEM)
    smem = pl.BlockSpec(memory_space=pltpu.SMEM)
    dma = pltpu.SemaphoreType.DMA
    bf16 = jnp.bfloat16
    transposed = pl.pallas_call(
        kernel,
        out_shape=jax.ShapeDtypeStruct((GROUP * COLS, BLK), bf16),
        in_specs=[vmem, vmem, vmem, vmem, smem, pl.BlockSpec(memory_space=pl.ANY)],
        out_specs=vmem,
        scratch_shapes=[
            pltpu.VMEM((NX * NY, depth, rows // NY), bf16),
            pltpu.VMEM((NX * NY, depth, 128), bf16),
            pltpu.VMEM((BLOCKS + 1, COLS, BLK), bf16),
            pltpu.VMEM((4, COLS, BLK), bf16),
            pltpu.VMEM((GROUP, SLOTS, BLK, BLK), bf16),
            pltpu.VMEM((GROUP, 8, 128), jnp.int32),
            pltpu.SMEM((GROUP, 8, 128), jnp.int32),
            pltpu.VMEM((128, 128), jnp.float32),
            pltpu.VMEM((GROUP, COLS, BLK), bf16),
            pltpu.VMEM((GROUP, COLS, BLK), bf16),
            dma((2, NX * NY - 1)),
            dma((2, NX * NY - 1)),
            dma((2, GROUP - 1)),
            dma((1,)),
            dma((2, 10)),
            dma((1,)),
            dma((2, 1)),
            dma((2, NY - 1)),
            dma((2, 2, NZ // 2)),
            dma((2, 2, NZ // 2)),
            dma((2, 2, NZ)),
            dma((2, 2, NZ)),
            dma((2, GROUP - 1)),
        ],
        compiler_params=pltpu.CompilerParams(
            collective_id=0, has_side_effects=True, vmem_limit_bytes=40 * 2**20
        ),
    )(ft, weight, bias.reshape(NX, 128), tile_src, tile_count, tile_vals)
    return transposed.T


def solution(mesh):
    placed = (
        P("node", "feat"),
        P("feat", None),
        P(),
        P(("node", "feat"), None),
        P(("node", "feat")),
        P(("node", "feat"), None, None, None),
    )
    return jax.shard_map(
        shards, mesh=mesh, in_specs=placed, out_specs=P(("node", "feat"), None), check_vma=False
    )
```

time: 510 us -> 130 us (0.25); the launches traced: 502 us -> 128 us
  waiting for transfers between devices: 393 us -> 0 us
  Pallas kernels: 0 us -> 123 us
  blocking collectives: 52.5 us -> 0 us
  starting transfers between devices: 21.6 us -> 0 us
  between operations: 14.1 us -> 0.7 us
  local copies, waits for them, and re-layouts: 15.2 us -> 3.61 us
    all_to_all x2 -> x0, waiting for transfers between devices: 361 us -> none  [the longest x1 361 us: shards(): lax.all_to_all(picked, 'node', split_axis=0, concat_axis=0, tiled=True)]
    pallas_call x0 -> x1, Pallas kernels: none -> 123 us  [shards(): pl.pallas_call(kernel, out_shape=jax.ShapeDtypeStruct((GROUP * COLS, BLK)...]
    all_to_all x1 -> x0, blocking collectives: 32.4 us -> none  [shards(): lax.all_to_all(requests, 'node', split_axis=0, concat_axis=0, tiled=True)]
    all_gather x1 -> x0, waiting for transfers between devices: 32.2 us -> none  [shards(): partition_rows = lax.all_gather(hidden, 'feat', axis=0, tiled=True)]
    all_to_all x2 -> x0, starting transfers between devices: 21.6 us -> none  [the longest x1 14 us: shards(): lax.all_to_all(picked, 'node', split_axis=0, concat_axis=0, tiled=True)]
    all_gather x1 -> x0, blocking collectives: 20.1 us -> none  [shards(): full_weight = lax.all_gather(weight, 'feat', axis=0, tiled=True)]
    gather x2 -> x0, local copies, waits for them, and re-layouts: 13.2 us -> none  [the longest x1 6.93 us: shards(): group_blocks[lax.all_to_all(requests, 'node', split_axis=0, concat_axis=0...]
  transfers between devices with their start and end apart: 3 -> 0, of which waited for: 2 -> 0; matrix products, arithmetic and copies ran while one was open for 0% -> 0% of each run, Pallas kernels for 0% -> 0%
where the time goes in v1:
time: 130 us; the launch traced here: 128 us
  Pallas kernels  123 us (95%)
  local copies, waits for them, and re-layouts  3.61 us (3%)
    pallas_call x1, Pallas kernels, shards(): pl.pallas_call(kernel, out_shape=jax.ShapeDtypeStruct((GROUP * COLS, BLK)...  123 us

profile of v1, /device:TPU:1, one launch (start us, length us, event | category | flops | bytes accessed | tf_op | source)
XLA Modules:
  0.0 127.6 jit_solution(1355945841773490399)
XLA Ops:
  0.7 0.0 copy-start.1
  0.7 1.0 copy.12
  1.6 0.0 copy-start.2
  1.6 0.0 copy-start.3
  1.6 0.0 copy-done.1
  1.7 0.7 copy-done.2
  2.3 0.0 copy-done.3
  2.3 0.0 copy-start
  2.3 1.2 copy-done
  3.5 123.3 %shard_map.64 = bf16[512,128]{1,0:T(8,128)(2,1)S(1)} custom-call(bf16[4,48,512]{2,1,0:T(8,128)(2,1)S(1)} %bitcast.9, bf16[48,512]{1,0:T(8,128)(2,1)S(1)} %copy-done.1, f32[4,128]{1,0:T(4,128)S(1)} %bitcast.11, s32[1,32]{1,0:T(1,128)S(1)} %copy-done.3, s32[1]{0:T(128)S(6)} %copy.13.cnt, bf16[1,32,128,128]{3,2,1,0:T(8,128)(2,1)S(1)} %copy-done), custom_call_target="tpu_custom_call" | custom-call | tf_op jit(solution)/shard_map/pallas_call | solution.py:353
  126.9 0.8 copy.9
Async XLA Ops:
  0.7 1.0 copy-start.1
  1.6 0.7 copy-start.2
  1.6 0.7 copy-start.3
  2.3 1.2 copy-start

commit v2 on v1

--- a/solution.py
+++ b/solution.py
@@ -153,9 +153,9 @@
 
     hz = hb.at[pl.ds(0, BLOCKS)].reshape(NZ, NY, SHARD, COLS, BLK)
 
-    def rz_copy(zz, step, direction, first=0, count=NY):
-        ref = hz.at[zz, pl.ds(first, count), pl.ds(PART, SHARD - PART)]
-        return remote(ref, ref, rz_sem, (direction, step), (above, below)[direction])
+    def rz_copy(zz, step, direction, part):
+        ref = hz.at[zz, pl.ds(part * (NY // 2), NY // 2), pl.ds(PART, SHARD - PART)]
+        return remote(ref, ref, rz_sem, (direction, part, step), (above, below)[direction])
 
     def py_copy(zz, yy, direction):
         ref = blocks(zz, yy, 0, PART)
@@ -174,39 +174,13 @@
     py_copy(z, y, 1).start()
     for j in range(1, NY):
         ry_copy(j).wait_recv()
-    rz_copy(z, 0, 0).start()
-    rz_copy(z, 0, 1).start()
-
-    def p_arrived(step):
-        lower, upper = down(z, NZ, step), up(z, NZ, step)
-        pz_copy(lower, step - 1, 0).wait_recv()
-        pz_copy(upper, step - 1, 1).wait_recv()
-        return lower, upper
-
-    @pl.loop(1, far - 1)
-    def _(step):
-        lower, upper = p_arrived(step)
-        pz_copy(lower, step, 0).start()
-        pz_copy(upper, step, 1).start()
-        for zz in (lower, upper):
-            py_copy(zz, y, 0).start()
-            py_copy(zz, y, 1).start()
-
-    lower, upper = p_arrived(far - 1)
-    pz_last = (
-        pz_copy(lower, far - 1, 0, 0, HALF),
-        pz_copy(upper, far - 1, 1, HALF, PART - HALF),
-    )
-    for copy in pz_last:
-        copy.start()
-    for zz in (lower, upper):
+    for part in range(2):
+        rz_copy(z, 0, 0, part).start()
+        rz_copy(z, 0, 1, part).start()
+
+    def spread(zz):
         py_copy(zz, y, 0).start()
         py_copy(zz, y, 1).start()
-    opposite = up(z, NZ, far)
-    pz_copy(opposite, far - 1, 0, 0, HALF).wait_recv()
-    pz_copy(opposite, far - 1, 1, HALF, PART - HALF).wait_recv()
-    py_copy(opposite, y, 0).start()
-    py_copy(opposite, y, 1).start()
 
     def pass_on(zz):
         py_copy(zz, down(y, NY), 0).wait_recv()
@@ -214,50 +188,66 @@
         py_copy(zz, up(y, NY), 1).wait_recv()
         pf_copy(zz, up(y, NY), 1).start()
 
-    def r_arrived(step):
+    def ring_step(step):
         lower, upper = down(z, NZ, step), up(z, NZ, step)
-        rz_copy(lower, step - 1, 0).wait_recv()
-        rz_copy(upper, step - 1, 1).wait_recv()
-        return lower, upper
-
-    def r_step(step):
-        lower, upper = r_arrived(step)
-        rz_copy(lower, step, 0).start()
-        rz_copy(upper, step, 1).start()
-        return lower, upper
-
+        pz_copy(lower, step - 1, 0).wait_recv()
+        pz_copy(lower, step, 0).start()
+        pz_copy(upper, step - 1, 1).wait_recv()
+        pz_copy(upper, step, 1).start()
+        spread(lower)
+        spread(upper)
+        for part in range(2):
+            rz_copy(lower, step - 1, 0, part).wait_recv()
+            rz_copy(lower, step, 0, part).start()
+            rz_copy(upper, step - 1, 1, part).wait_recv()
+            rz_copy(upper, step, 1, part).start()
+
+    ring_step(1)
     pass_on(z)
-    pass_on(opposite)
-
-    def both(step):
-        lower, upper = r_step(step)
-        pass_on(lower)
-        pass_on(upper)
-
-    @pl.loop(1, 4)
+
+    @pl.loop(2, far - 1)
     def _(step):
-        both(step)
-
-    t_low_right.wait_recv()
-    t_pass_right.start()
-    t_high_left.wait_recv()
-    t_pass_left.start()
-    t_high_right.wait_recv()
-    t_sibling[0].start()
-    t_low_left.wait_recv()
-    t_sibling[1].start()
-
-    @pl.loop(4, far - 1)
-    def _(step):
-        both(step)
-
-    lower, upper = r_arrived(far - 1)
-    rz_last = (
-        rz_copy(lower, far - 1, 0, 0, NY // 2),
-        rz_copy(upper, far - 1, 1, NY // 2, NY // 2),
+        ring_step(step)
+        pass_on(down(z, NZ, step - 1))
+        pass_on(up(z, NZ, step - 1))
+
+        @pl.when(step == 4)
+        def _():
+            t_low_right.wait_recv()
+            t_pass_right.start()
+            t_high_left.wait_recv()
+            t_pass_left.start()
+
+        @pl.when(step == 5)
+        def _():
+            t_high_right.wait_recv()
+            t_sibling[0].start()
+            t_low_left.wait_recv()
+            t_sibling[1].start()
+
+    lower, upper, opposite = down(z, NZ, far - 1), up(z, NZ, far - 1), up(z, NZ, far)
+    pz_last = (
+        pz_copy(lower, far - 1, 0, 0, HALF),
+        pz_copy(upper, far - 1, 1, HALF, PART - HALF),
     )
-    for copy in rz_last:
-        copy.start()
+    rz_last = (rz_copy(lower, far - 1, 0, 0), rz_copy(upper, far - 1, 1, 1))
+    pz_copy(lower, far - 2, 0).wait_recv()
+    pz_last[0].start()
+    pz_copy(upper, far - 2, 1).wait_recv()
+    pz_last[1].start()
+    spread(lower)
+    spread(upper)
+    rz_copy(lower, far - 2, 0, 0).wait_recv()
+    rz_last[0].start()
+    rz_copy(upper, far - 2, 1, 1).wait_recv()
+    rz_last[1].start()
+    rz_copy(lower, far - 2, 0, 1).wait_recv()
+    rz_copy(upper, far - 2, 1, 0).wait_recv()
+    pass_on(down(z, NZ, far - 2))
+    pass_on(up(z, NZ, far - 2))
+    pz_copy(opposite, far - 1, 0, 0, HALF).wait_recv()
+    pz_copy(opposite, far - 1, 1, HALF, PART - HALF).wait_recv()
+    spread(opposite)
     pass_on(lower)
     pass_on(upper)
 
@@ -265,8 +255,9 @@
     remote(tbuf.at[from_far, high], tbuf.at[from_far, high], t_sem, (6,), left).wait_recv()
     t_sibling[2].start()
 
-    rz_copy(opposite, far - 1, 0, 0, NY // 2).wait_recv()
-    rz_copy(opposite, far - 1, 1, NY // 2, NY // 2).wait_recv()
+    rz_copy(opposite, far - 1, 0, 0).wait_recv()
+    rz_copy(opposite, far - 1, 1, 1).wait_recv()
+    pass_on(opposite)
 
     @pl.loop(0, NZ)
     def _(zz):
@@ -324,7 +315,8 @@
     def _(step):
         for direction in range(2):
             pz_copy(z, step, direction).wait_send()
-            rz_copy(z, step, direction).wait_send()
+            rz_copy(z, step, direction, 0).wait_send()
+            rz_copy(z, step, direction, 1).wait_send()
 
     @pl.loop(0, NZ)
     def _(zz):
@@ -375,7 +367,7 @@
             dma((2, 1)),
             dma((2, NY - 1)),
             dma((2, 2, NZ // 2)),
-            dma((2, 2, NZ // 2)),
+            dma((2, 2, 2, NZ // 2)),
             dma((2, 2, NZ)),
             dma((2, 2, NZ)),
             dma((2, GROUP - 1)),

time: 130 us -> 104 us (0.80); the launches traced: 128 us -> 104 us
  Pallas kernels: 123 us -> 99.9 us
    pallas_call x1, Pallas kernels: 123 us -> 99.9 us  [shards(): pl.pallas_call(kernel, out_shape=jax.ShapeDtypeStruct((GROUP * COLS, BLK)...]
where the time goes in v2:
time: 104 us
  Pallas kernels  99.9 us (96%)
  local copies, waits for them, and re-layouts  3.61 us (3%)
    pallas_call x1, Pallas kernels, shards(): pl.pallas_call(kernel, out_shape=jax.ShapeDtypeStruct((GROUP * COLS, BLK)...  99.9 us

profile of v2, /device:TPU:1, one launch (start us, length us, event | category | flops | bytes accessed | tf_op | source)
XLA Modules:
  0.0 104.2 jit_solution(12311614781668087683)
XLA Ops:
  0.7 0.0 copy-start.1
  0.7 1.0 copy.12
  1.6 0.0 copy-start.2
  1.6 0.0 copy-start.3
  1.6 0.0 copy-done.1
  1.7 0.7 copy-done.2
  2.3 0.0 copy-done.3
  2.3 0.0 copy-start
  2.3 1.2 %copy-done = bf16[1,32,128,128]{3,2,1,0:T(8,128)(2,1)S(1)} copy-done((bf16[1,32,128,128]{3,2,1,0:T(8,128)(2,1)S(1)}, bf16[1,32,128,128]{3,2,1,0:T(8,128)(2,1)}, u32[]{:S(2)}) %copy-start) | copy-done | bytes 1048600
  3.5 99.9 %shard_map.64 = bf16[512,128]{1,0:T(8,128)(2,1)S(1)} custom-call(bf16[4,48,512]{2,1,0:T(8,128)(2,1)S(1)} %bitcast.9, bf16[48,512]{1,0:T(8,128)(2,1)S(1)} %copy-done.1, f32[4,128]{1,0:T(4,128)S(1)} %bitcast.11, s32[1,32]{1,0:T(1,128)S(1)} %copy-done.3, s32[1]{0:T(128)S(6)} %copy.13.cnt, bf16[1,32,128,128]{3,2,1,0:T(8,128)(2,1)S(1)} %copy-done), custom_call_target="tpu_custom_call" | custom-call | tf_op jit(solution)/shard_map/pallas_call | solution.py:345
  103.4 0.8 copy.9
Async XLA Ops:
  0.7 1.0 copy-start.1
  1.6 0.7 copy-start.2
  1.6 0.7 copy-start.3
  2.3 1.2 %copy-start = (bf16[1,32,128,128]{3,2,1,0:T(8,128)(2,1)S(1)}, bf16[1,32,128,128]{3,2,1,0:T(8,128)(2,1)}, u32[]{:S(2)}) copy-start(bf16[1,32,128,128]{3,2,1,0:T(8,128)(2,1)} %tiles.1) | copy-start | bytes 3145732

commit v3 on v2

v3 whole, which is shorter than its diff:
```python
import jax
import jax.numpy as jnp
from jax import lax
from jax.experimental import pallas as pl
from jax.experimental.pallas import tpu as pltpu
from jax.sharding import PartitionSpec as P

MESH = pl.DeviceIdType.MESH
NX, NY, NZ = 4, 4, 16
BLK = 128
COLS = 64
GROUP = 2 * NX
PART = 5
SHARD = 8
HALF = 3
BLOCKS = NZ * NY * SHARD
SLOTS = 32
UNROLL = 8
ROWS = 512
ORDER = (
    "R0 R1 P1 R2", "Y0 R3 R4 P2", "R5 Y1 R6 R7", "P3 R8 Y2 R9",
    "R10 P4 R11 R12", "Y3 R13 P5 T0", "R14 R15 Y4 R16", "P6 R17 R18 Y5",
    "R19 P7 T1 R20", "R21 R22 P8 R23", "R24 Y6 R25 R26", "Y7 R27 Y8 R28",
    "R30 R29 R31",
)
PLANE = (
    (2, 2), (2, 1), (1, 2), (2, 3), (3, 2), (1, 1), (3, 3), (1, 3), (3, 1), (2, 0), (0, 2), (1, 0), (3, 0), (0, 1), (0, 3),
)


def kernel(
    ft, w, bias, src, cnt, tiles, out,
    xbuf, wbuf, hb, stage, tbuf, sv, ss, bt, obuf, rbuf,
    bv, iv, x_sem, w_sem, s_sem, ss_sem, t_sem, local_sem, h_sem, ry_sem, pz_sem, rz_sem, py_sem, pf_sem, o_sem,
):
    n = lax.axis_index("node")
    f = lax.axis_index("feat")
    z, c = lax.div(n, 2), lax.rem(n, 2)
    x, y = lax.div(f, NY), lax.rem(f, NY)
    me = x * 2 + c

    def at(xx, yy, zz, cc):
        return (zz * 2 + cc, xx * NY + yy)

    def up(value, size, by=1):
        return lax.rem(value + by, size)

    def down(value, size, by=1):
        return lax.rem(value + size - by, size)

    def remote(source, target, sems, index, device):
        return pltpu.make_async_remote_copy(
            src_ref=source, dst_ref=target, send_sem=sems.at[(0,) + index], recv_sem=sems.at[(1,) + index],
            device_id=device, device_id_type=MESH,
        )

    sibling = at(x, y, z, 1 - c)
    right, left = at(up(x, NX), y, z, c), at(down(x, NX), y, z, c)
    front, back = at(x, up(y, NY), z, c), at(x, down(y, NY), z, c)
    above, below = at(x, y, up(z, NZ), c), at(x, y, down(z, NZ), c)

    def group_peer(i):
        dx, dc = lax.rem(1 + lax.div(i, 2), NX), 1 - lax.rem(i, 2)
        xx, cc = up(x, NX, dx), lax.rem(c + dc, 2)
        return xx * 2 + cc, at(xx, y, z, cc)

    def group_source(i):
        dx, dc = lax.rem(1 + lax.div(i, 2), NX), 1 - lax.rem(i, 2)
        return down(x, NX, dx) * 2 + lax.rem(c + dc, 2)

    barrier = pltpu.get_barrier_semaphore()

    @pl.loop(1, NX * NY)
    def _(i):
        pl.semaphore_signal(barrier, inc=1, device_id=(n, lax.rem(f + i, NX * NY)), device_id_type=MESH)

    for i in range(1, NX):
        pl.semaphore_signal(barrier, inc=1, device_id=at(up(x, NX, i), y, z, 1 - c), device_id_type=MESH)
    for device in (sibling, above, below):
        pl.semaphore_signal(barrier, inc=1, device_id=device, device_id_type=MESH)

    local = [
        pltpu.make_async_copy(source, target, local_sem.at[i])
        for i, (source, target) in enumerate((
            (tiles.at[0], tbuf.at[me]),
            (bias, bv),
            (src, iv),
            (ft.at[:, pl.ds(pl.multiple_of(y * ROWS, ROWS), ROWS)], xbuf.at[f]),
            (w.at[:, pl.ds(pl.multiple_of(x * 128, 128), 128)], wbuf.at[f]),
        ))
    ]
    for copy in local:
        copy.start()

    hb[BLOCKS] = jnp.zeros((COLS, BLK), jnp.bfloat16)
    local[1].wait()
    bt[...] = jnp.broadcast_to(bv[pl.ds(x, 1), :], (128, 128)).T
    local[2].wait()
    s = iv[...]
    zz, rest = lax.shift_right_logical(s, 5), s & 31
    cc, ff = lax.shift_right_logical(rest, 4), rest & 15
    place = (zz * NY + lax.shift_right_logical(ff, 2)) * SHARD + cc * 4 + (ff & 3)
    alive = lax.broadcasted_iota(jnp.int32, s.shape, 1) < cnt[0]
    sv[me] = jnp.zeros((8, 128), jnp.int32)
    sv[me, 0:1, 0:SLOTS] = jnp.where(alive, place, BLOCKS)

    pl.semaphore_wait(barrier, NX * NY - 1 + NX - 1 + 3)

    def plane_copies(i):
        dx, dy = PLANE[i]
        xx, yy = up(x, NX, dx), up(y, NY, dy)
        rows = pl.ds(pl.multiple_of(yy * ROWS, ROWS), ROWS)
        columns = pl.ds(pl.multiple_of(xx * 128, 128), 128)
        device = at(xx, yy, z, c)
        return (
            remote(ft.at[:, rows], xbuf.at[f], x_sem, (i,), device),
            remote(w.at[:, columns], wbuf.at[f], w_sem, (i,), device),
        )

    plane = [copy for i in range(len(PLANE)) for copy in plane_copies(i)]
    for copy in plane:
        copy.start()

    def s_copy(i):
        _, device = group_peer(i)
        return remote(sv.at[me], sv.at[me], s_sem, (i,), device)

    for i in range(GROUP - 1):
        s_copy(i).start()
    local[3].wait()
    local[4].wait()
    for copy in plane:
        copy.wait_recv()

    own = tiles.at[0]
    low, high = pl.ds(0, SLOTS // 2), pl.ds(SLOTS // 2, SLOTS // 2)
    t_low_right = remote(own.at[low], tbuf.at[me, low], t_sem, (0,), right)
    t_high_left = remote(own.at[high], tbuf.at[me, high], t_sem, (1,), left)
    t_high_right = remote(own.at[high], tbuf.at[me, high], t_sem, (2,), right)
    t_low_left = remote(own.at[low], tbuf.at[me, low], t_sem, (3,), left)
    t_own_sibling = remote(own, tbuf.at[me], t_sem, (4,), sibling)
    for copy in (t_low_right, t_high_left, t_high_right, t_low_left, t_own_sibling):
        copy.start()
    from_left, from_right, from_far = (down(x, NX) * 2 + c, up(x, NX) * 2 + c, up(x, NX, 2) * 2 + c)
    t_pass_right = remote(tbuf.at[from_left, low], tbuf.at[from_left, low], t_sem, (5,), right)
    t_pass_left = remote(tbuf.at[from_right, high], tbuf.at[from_right, high], t_sem, (6,), left)
    t_sibling = [
        remote(tbuf.at[e], tbuf.at[e], t_sem, (7 + j,), sibling)
        for j, e in enumerate((from_left, from_right, from_far))
    ]

    ht = lax.dot_general(
        wbuf[...].reshape(NX * NY * 48, 128), xbuf[...].reshape(NX * NY * 48, 512),
        (((0,), (0,)), ((), ())), preferred_element_type=jnp.float32,
    ).astype(jnp.bfloat16)
    mine = jnp.where(c == 0, ht[:COLS], ht[COLS:])
    other = jnp.where(c == 0, ht[COLS:], ht[:COLS])
    place_of = lambda zz, yy: (zz * NY + yy) * SHARD
    base = place_of(z, y) + c * 4
    for k in range(4):
        stage[k] = other[:, k * BLK : (k + 1) * BLK]
    h_copy = remote(stage, hb.at[pl.ds(base, 4)], h_sem, (0,), sibling)
    h_copy.start()
    for k in range(4):
        hb[base + k] = mine[:, k * BLK : (k + 1) * BLK]
    h_copy.wait_recv()

    def blocks(zz, yy, first, count):
        return hb.at[pl.ds(place_of(zz, yy) + first, count)]

    def ry_copy(j):
        ref = blocks(z, y, PART, SHARD - PART)
        return remote(ref, ref, ry_sem, (j - 1,), at(x, up(y, NY, j), z, c))

    def pz_copy(zz, step, direction, first=0, count=PART):
        ref = blocks(zz, y, first, count)
        return remote(ref, ref, pz_sem, (direction, step), (above, below)[direction])

    def rz_copy(step, j, direction):
        zz = down(z, NZ, step) if direction == 0 else up(z, NZ, step)
        ref = blocks(zz, down(y, NY, j), PART, SHARD - PART)
        return remote(ref, ref, rz_sem, (direction, j, step), (above, below)[direction])

    def py_copy(zz, yy, direction):
        ref = blocks(zz, yy, 0, PART)
        return remote(ref, ref, py_sem, (direction, zz), (front, back)[direction])

    def pf_copy(zz, yy, direction, first):
        ref = blocks(zz, yy, *((0, HALF) if direction == first else (HALF, PART - HALF)))
        return remote(ref, ref, pf_sem, (direction, zz), (front, back)[direction])

    far = NZ // 2
    lower = [down(z, NZ, step) for step in range(far + 1)]
    upper = [up(z, NZ, step) for step in range(far + 1)]

    def p_copies(step):
        if step < far - 1:
            return [pz_copy(lower[step], step, 0), pz_copy(upper[step], step, 1)]
        return [pz_copy(lower[step], step, 0, 0, HALF), pz_copy(upper[step], step, 1, HALF, PART - HALF)]

    def r_copies(step, j):
        return [rz_copy(step, j, direction) for direction in range(2) if step < far - 1 or j // 2 == direction]

    def places_at(step):
        return [(lower[step], 0)] if step in (0, far) else [(lower[step], 0), (upper[step], 1)]

    def spread(step):
        for zz, _ in places_at(step):
            for direction in range(2):
                py_copy(zz, y, direction).start()

    def p_step(step):
        sends = p_copies(step) if step < far else [None, None]
        for arrival, send in zip(p_copies(step - 1), sends):
            arrival.wait_recv()
            if send is not None:
                send.start()
        spread(step)

    def r_step(q):
        step, j = q // NY, q % NY
        if step == 0 and j > 0:
            ry_copy(j).wait_recv()
        if step > 0:
            for copy in r_copies(step - 1, j):
                copy.wait_recv()
        if step < far:
            for copy in r_copies(step, j):
                copy.start()

    def y_step(step):
        for zz, first in places_at(step):
            for direction, yy in ((0, down(y, NY)), (1, up(y, NY))):
                py_copy(zz, yy, direction).wait_recv()
                pf_copy(zz, yy, direction, first).start()

    def t_step(part):
        if part == 0:
            t_low_right.wait_recv()
            t_pass_right.start()
            t_high_left.wait_recv()
            t_pass_left.start()
        else:
            t_high_right.wait_recv()
            t_sibling[0].start()
            t_low_left.wait_recv()
            t_sibling[1].start()

    for j in range(1, NY):
        ry_copy(j).start()
    for copy in p_copies(0):
        copy.start()
    spread(0)
    steps = {"P": p_step, "R": r_step, "Y": y_step, "T": t_step}
    for entry in " ".join(ORDER).split():
        steps[entry[0]](int(entry[1:]))
    for j in range(NY):
        for copy in r_copies(far - 1, j):
            copy.wait_recv()

    remote(tbuf.at[from_far, low], tbuf.at[from_far, low], t_sem, (5,), right).wait_recv()
    remote(tbuf.at[from_far, high], tbuf.at[from_far, high], t_sem, (6,), left).wait_recv()
    t_sibling[2].start()
    for step in range(far + 1):
        for zz, first in places_at(step):
            for direction in range(2):
                pf_copy(zz, up(y, NY, 2), direction, first).wait_recv()

    for i in range(GROUP - 1):
        s_copy(i).wait_recv()
    places = pltpu.make_async_copy(sv, ss, ss_sem.at[0])
    places.start()
    local[0].wait()
    t_own_sibling.wait_recv()
    for copy in t_sibling:
        copy.wait_recv()
    places.wait()

    def aggregate(e):
        total = jnp.zeros((COLS, BLK), jnp.float32)
        for first in range(0, SLOTS, UNROLL):
            slots = range(first, first + UNROLL)
            picked = jnp.concatenate([hb[ss[e, 0, t]] for t in slots], axis=1)
            values = jnp.concatenate([tbuf[e, t] for t in slots], axis=1)
            total += lax.dot_general(
                picked, values, (((1,), (1,)), ((), ())), preferred_element_type=jnp.float32
            )
        return jnp.maximum(total + bt[pl.ds(pl.multiple_of(c * COLS, COLS), COLS), :], 0.0).astype(jnp.bfloat16)

    def o_copy(i):
        _, device = group_peer(i)
        return remote(obuf.at[i], rbuf.at[me], o_sem, (i,), device)

    @pl.loop(0, GROUP - 1)
    def _(i):
        e, _ = group_peer(i)
        obuf[i] = aggregate(e)
        o_copy(i).start()

    rbuf[me] = aggregate(me)

    for copy in plane:
        copy.wait_send()

    for i in range(GROUP - 1):
        s_copy(i).wait_send()
    for copy in (t_low_right, t_high_left, t_high_right, t_low_left, t_own_sibling, t_pass_right, t_pass_left, h_copy):
        copy.wait_send()
    for copy in t_sibling:
        copy.wait_send()
    for j in range(1, NY):
        ry_copy(j).wait_send()

    for step in range(far):
        for copy in p_copies(step):
            copy.wait_send()
        for j in range(NY):
            for copy in r_copies(step, j):
                copy.wait_send()
    for step in range(far + 1):
        for zz, first in places_at(step):
            for direction in range(2):
                py_copy(zz, y, direction).wait_send()
                pf_copy(zz, y, direction, first).wait_send()

    @pl.loop(0, GROUP - 1)
    def _(i):
        o_copy(i).wait_recv()

    out[...] = rbuf[...].reshape(GROUP * COLS, BLK)

    @pl.loop(0, GROUP - 1)
    def _(i):
        o_copy(i).wait_send()


def shards(features, weight, bias, tile_src, tile_count, tile_vals):
    rows, depth = features.shape
    vmem = pl.BlockSpec(memory_space=pltpu.VMEM)
    hbm = pl.BlockSpec(memory_space=pltpu.HBM)
    smem = pl.BlockSpec(memory_space=pltpu.SMEM)
    dma = pltpu.SemaphoreType.DMA
    bf16 = jnp.bfloat16
    transposed = pl.pallas_call(
        kernel,
        out_shape=jax.ShapeDtypeStruct((GROUP * COLS, BLK), bf16),
        in_specs=[hbm, hbm, hbm, hbm, smem, hbm],
        out_specs=vmem,
        scratch_shapes=[
            pltpu.VMEM((NX * NY, depth, rows // NY), bf16),
            pltpu.VMEM((NX * NY, depth, 128), bf16),
            pltpu.VMEM((BLOCKS + 1, COLS, BLK), bf16),
            pltpu.VMEM((4, COLS, BLK), bf16),
            pltpu.VMEM((GROUP, SLOTS, BLK, BLK), bf16),
            pltpu.VMEM((GROUP, 8, 128), jnp.int32),
            pltpu.SMEM((GROUP, 8, 128), jnp.int32),
            pltpu.VMEM((128, 128), jnp.float32),
            pltpu.VMEM((GROUP, COLS, BLK), bf16),
            pltpu.VMEM((GROUP, COLS, BLK), bf16),
            pltpu.VMEM((NX, 128), jnp.float32),
            pltpu.VMEM((1, SLOTS), jnp.int32),
            dma((2, NX * NY - 1)),
            dma((2, NX * NY - 1)),
            dma((2, GROUP - 1)),
            dma((1,)),
            dma((2, 10)),
            dma((5,)),
            dma((2, 1)),
            dma((2, NY - 1)),
            dma((2, 2, NZ // 2)),
            dma((2, 2, NY, NZ // 2)),
            dma((2, 2, NZ)),
            dma((2, 2, NZ)),
            dma((2, GROUP - 1)),
        ],
        compiler_params=pltpu.CompilerParams(
            collective_id=0, has_side_effects=True, vmem_limit_bytes=56 * 2**20
        ),
    )(features.T, weight, bias.reshape(NX, 128), tile_src, tile_count, tile_vals)
    return transposed.T


def solution(mesh):
    placed = (
        P("node", "feat"),
        P("feat", None),
        P(),
        P(("node", "feat"), None),
        P(("node", "feat")),
        P(("node", "feat"), None, None, None),
    )
    return jax.shard_map(
        shards, mesh=mesh, in_specs=placed, out_specs=P(("node", "feat"), None), check_vma=False
    )
```

time: 104 us -> 94.7 us (0.911)
  Pallas kernels: 99.9 us -> 92.3 us
  local copies, waits for them, and re-layouts: 3.61 us -> 1.67 us
    pallas_call x1, Pallas kernels: 99.9 us -> 92.3 us  [shards(): pl.pallas_call(kernel, out_shape=jax.ShapeDtypeStruct((GROUP * COLS, BLK)...]
    unnamed x8 -> x0, local copies, waits for them, and re-layouts: 1.89 us -> none
where the time goes in v3:
time: 94.7 us; the launch traced here: 94.6 us
  Pallas kernels  92.3 us (97%)
  local copies, waits for them, and re-layouts  1.67 us (2%)
    pallas_call x1, Pallas kernels, shards(): pl.pallas_call(kernel, out_shape=jax.ShapeDtypeStruct((GROUP * COLS, BLK)...  92.3 us

profile of v3, /device:TPU:1, one launch (start us, length us, event | category | flops | bytes accessed | tf_op | source)
XLA Modules:
  0.0 94.6 jit_solution(11705766241518724392)
XLA Ops:
  0.7 92.3 %shard_map.64 = bf16[512,128]{1,0:T(8,128)(2,1)} custom-call(bf16[48,2048]{1,0:T(8,128)(2,1)} %bitcast.4, bf16[48,512]{1,0:T(8,128)(2,1)} %w.1, f32[4,128]{1,0:T(4,128)} %bitcast.5, s32[1,32]{1,0:T(1,128)} %src.1, s32[1]{0:T(128)S(6)} %copy.8.cnt, bf16[1,32,128,128]{3,2,1,0:T(8,128)(2,1)} %tiles.1), custom_call_target="tpu_custom_call" | custom-call | tf_op jit(solution)/shard_map/pallas_call | solution.py:344
  92.9 1.7 %copy.7 = bf16[128,512]{1,0:T(8,128)(2,1)} copy(bf16[128,512]{0,1:T(8,128)(2,1)} %bitcast.3) | data formatting | bytes 262144 | tf_op jit(solution)/shard_map/transpose | solution.py:380

commit v4 on v3

--- a/solution.py
+++ b/solution.py
@@ -20,8 +20,8 @@
 ORDER = (
     "R0 R1 P1 R2", "Y0 R3 R4 P2", "R5 Y1 R6 R7", "P3 R8 Y2 R9",
     "R10 P4 R11 R12", "Y3 R13 P5 T0", "R14 R15 Y4 R16", "P6 R17 R18 Y5",
-    "R19 P7 T1 R20", "R21 R22 P8 R23", "R24 Y6 R25 R26", "Y7 R27 Y8 R28",
-    "R30 R29 R31",
+    "R19 P7 T1 R20", "R21 R22 P8 R23", "R24 Y6 R25 R26", "T2 Y7 R27 Y8",
+    "R28 R30 R29 R31",
 )
 PLANE = (
     (2, 2), (2, 1), (1, 2), (2, 3), (3, 2), (1, 1), (3, 3), (1, 3), (3, 1), (2, 0), (0, 2), (1, 0), (3, 0), (0, 1), (0, 3),
@@ -31,7 +31,7 @@
 def kernel(
     ft, w, bias, src, cnt, tiles, out,
     xbuf, wbuf, hb, stage, tbuf, sv, ss, bt, obuf, rbuf,
-    bv, iv, x_sem, w_sem, s_sem, ss_sem, t_sem, local_sem, h_sem, ry_sem, pz_sem, rz_sem, py_sem, pf_sem, o_sem,
+    bv, iv, x_sem, w_sem, v_sem, s_sem, ss_sem, t_sem, local_sem, h_sem, ry_sem, pz_sem, rz_sem, py_sem, pf_sem, o_sem,
 ):
     n = lax.axis_index("node")
     f = lax.axis_index("feat")
@@ -92,6 +92,35 @@
     for copy in local:
         copy.start()
 
+    pl.semaphore_wait(barrier, NX * NY - 1 + NX - 1 + 3)
+
+    def plane_peer(i):
+        dx, dy = PLANE[i]
+        return up(x, NX, dx), up(y, NY, dy)
+
+    def x_copy(i):
+        xx, yy = plane_peer(i)
+        rows = pl.ds(pl.multiple_of(yy * ROWS, ROWS), ROWS)
+        return remote(ft.at[:, rows], xbuf.at[f], x_sem, (i,), at(xx, yy, z, c))
+
+    def w_copy(i):
+        xx, yy = plane_peer(i)
+        columns = pl.ds(pl.multiple_of(xx * 128, 128), 128)
+        return remote(w.at[:, columns], wbuf.at[f], w_sem, (i,), at(xx, yy, z, c))
+
+    def w_shares(method):
+        for core in range(2):
+
+            @pl.when(c == core)
+            def _():
+                for i in range(core, len(PLANE), 2):
+                    method(i)
+
+    w_shares(lambda i: w_copy(i).start())
+    x_plane = [x_copy(i) for i in range(len(PLANE))]
+    for copy in x_plane:
+        copy.start()
+
     hb[BLOCKS] = jnp.zeros((COLS, BLK), jnp.bfloat16)
     local[1].wait()
     bt[...] = jnp.broadcast_to(bv[pl.ds(x, 1), :], (128, 128)).T
@@ -104,23 +133,6 @@
     sv[me] = jnp.zeros((8, 128), jnp.int32)
     sv[me, 0:1, 0:SLOTS] = jnp.where(alive, place, BLOCKS)
 
-    pl.semaphore_wait(barrier, NX * NY - 1 + NX - 1 + 3)
-
-    def plane_copies(i):
-        dx, dy = PLANE[i]
-        xx, yy = up(x, NX, dx), up(y, NY, dy)
-        rows = pl.ds(pl.multiple_of(yy * ROWS, ROWS), ROWS)
-        columns = pl.ds(pl.multiple_of(xx * 128, 128), 128)
-        device = at(xx, yy, z, c)
-        return (
-            remote(ft.at[:, rows], xbuf.at[f], x_sem, (i,), device),
-            remote(w.at[:, columns], wbuf.at[f], w_sem, (i,), device),
-        )
-
-    plane = [copy for i in range(len(PLANE)) for copy in plane_copies(i)]
-    for copy in plane:
-        copy.start()
-
     def s_copy(i):
         _, device = group_peer(i)
         return remote(sv.at[me], sv.at[me], s_sem, (i,), device)
@@ -129,8 +141,25 @@
         s_copy(i).start()
     local[3].wait()
     local[4].wait()
-    for copy in plane:
+    def hand_on(i):
+        dx, dy = PLANE[i]
+        ref = wbuf.at[down(x, NX, dx) * NY + down(y, NY, dy)]
+        return remote(ref, ref, v_sem, (i,), sibling)
+
+    def pass_weights(i):
+        w_copy(i).wait_recv()
+        hand_on(i).start()
+
+    w_shares(pass_weights)
+    for copy in x_plane:
         copy.wait_recv()
+    for core in range(2):
+
+        @pl.when(c == core)
+        def _():
+            for i in range(1 - core, len(PLANE), 2):
+                hand_on(i).wait_recv()
+
 
     own = tiles.at[0]
     low, high = pl.ds(0, SLOTS // 2), pl.ds(SLOTS // 2, SLOTS // 2)
@@ -139,7 +168,7 @@
     t_high_right = remote(own.at[high], tbuf.at[me, high], t_sem, (2,), right)
     t_low_left = remote(own.at[low], tbuf.at[me, low], t_sem, (3,), left)
     t_own_sibling = remote(own, tbuf.at[me], t_sem, (4,), sibling)
-    for copy in (t_low_right, t_high_left, t_high_right, t_low_left, t_own_sibling):
+    for copy in (t_low_right, t_high_left, t_high_right, t_low_left):
         copy.start()
     from_left, from_right, from_far = (down(x, NX) * 2 + c, up(x, NX) * 2 + c, up(x, NX, 2) * 2 + c)
     t_pass_right = remote(tbuf.at[from_left, low], tbuf.at[from_left, low], t_sem, (5,), right)
@@ -148,6 +177,10 @@
         remote(tbuf.at[e], tbuf.at[e], t_sem, (7 + j,), sibling)
         for j, e in enumerate((from_left, from_right, from_far))
     ]
+
+    t_from_right = remote(tbuf.at[from_far, low], tbuf.at[from_far, low], t_sem, (5,), right)
+    t_from_left = remote(tbuf.at[from_far, high], tbuf.at[from_far, high], t_sem, (6,), left)
+    places = pltpu.make_async_copy(sv, ss, ss_sem.at[0])
 
     ht = lax.dot_general(
         wbuf[...].reshape(NX * NY * 48, 128), xbuf[...].reshape(NX * NY * 48, 512),
@@ -161,6 +194,7 @@
         stage[k] = other[:, k * BLK : (k + 1) * BLK]
     h_copy = remote(stage, hb.at[pl.ds(base, 4)], h_sem, (0,), sibling)
     h_copy.start()
+    t_own_sibling.start()
     for k in range(4):
         hb[base + k] = mine[:, k * BLK : (k + 1) * BLK]
     h_copy.wait_recv()
@@ -208,6 +242,19 @@
         for zz, _ in places_at(step):
             for direction in range(2):
                 py_copy(zz, y, direction).start()
+
+    def p_sent(step):
+        for copy in p_copies(step):
+            copy.wait_send()
+
+    def r_sent(q):
+        for copy in r_copies(q // NY, q % NY):
+            copy.wait_send()
+
+    def y_sent(step):
+        for zz, first in places_at(step):
+            for direction in range(2):
+                pf_copy(zz, y, direction, first).wait_send()
 
     def p_step(step):
         sends = p_copies(step) if step < far else [None, None]
@@ -216,6 +263,8 @@
             if send is not None:
                 send.start()
         spread(step)
+        if step >= 2:
+            p_sent(step - 2)
 
     def r_step(q):
         step, j = q // NY, q % NY
@@ -227,12 +276,19 @@
         if step < far:
             for copy in r_copies(step, j):
                 copy.start()
+        if q >= 8:
+            r_sent(q - 8)
 
     def y_step(step):
         for zz, first in places_at(step):
             for direction, yy in ((0, down(y, NY)), (1, up(y, NY))):
                 py_copy(zz, yy, direction).wait_recv()
                 pf_copy(zz, yy, direction, first).start()
+        for zz, _ in places_at(step):
+            for direction in range(2):
+                py_copy(zz, y, direction).wait_send()
+        if step >= 2:
+            y_sent(step - 2)
 
     def t_step(part):
         if part == 0:
@@ -240,11 +296,23 @@
             t_pass_right.start()
             t_high_left.wait_recv()
             t_pass_left.start()
-        else:
+        elif part == 1:
             t_high_right.wait_recv()
             t_sibling[0].start()
             t_low_left.wait_recv()
             t_sibling[1].start()
+            for i in range(GROUP - 1):
+                s_copy(i).wait_recv()
+            places.start()
+        else:
+            t_from_right.wait_recv()
+            t_from_left.wait_recv()
+            t_sibling[2].start()
+            local[0].wait()
+            t_own_sibling.wait_recv()
+            for copy in t_sibling[:2]:
+                copy.wait_recv()
+            places.wait()
 
     for j in range(1, NY):
         ry_copy(j).start()
@@ -258,23 +326,12 @@
         for copy in r_copies(far - 1, j):
             copy.wait_recv()
 
-    remote(tbuf.at[from_far, low], tbuf.at[from_far, low], t_sem, (5,), right).wait_recv()
-    remote(tbuf.at[from_far, high], tbuf.at[from_far, high], t_sem, (6,), left).wait_recv()
-    t_sibling[2].start()
     for step in range(far + 1):
         for zz, first in places_at(step):
             for direction in range(2):
                 pf_copy(zz, up(y, NY, 2), direction, first).wait_recv()
 
-    for i in range(GROUP - 1):
-        s_copy(i).wait_recv()
-    places = pltpu.make_async_copy(sv, ss, ss_sem.at[0])
-    places.start()
-    local[0].wait()
-    t_own_sibling.wait_recv()
-    for copy in t_sibling:
-        copy.wait_recv()
-    places.wait()
+    t_sibling[2].wait_recv()
 
     def aggregate(e):
         total = jnp.zeros((COLS, BLK), jnp.float32)
@@ -299,8 +356,14 @@
 
     rbuf[me] = aggregate(me)
 
-    for copy in plane:
+    for copy in x_plane:
         copy.wait_send()
+
+    def w_over(i):
+        w_copy(i).wait_send()
+        hand_on(i).wait_send()
+
+    w_shares(w_over)
 
     for i in range(GROUP - 1):
         s_copy(i).wait_send()
@@ -311,23 +374,17 @@
     for j in range(1, NY):
         ry_copy(j).wait_send()
 
-    for step in range(far):
-        for copy in p_copies(step):
-            copy.wait_send()
-        for j in range(NY):
-            for copy in r_copies(step, j):
-                copy.wait_send()
-    for step in range(far + 1):
-        for zz, first in places_at(step):
-            for direction in range(2):
-                py_copy(zz, y, direction).wait_send()
-                pf_copy(zz, y, direction, first).wait_send()
+    p_sent(far - 1)
+    for q in range(NY * far - 8, NY * far):
+        r_sent(q)
+    for step in (far - 1, far):
+        y_sent(step)
 
     @pl.loop(0, GROUP - 1)
     def _(i):
         o_copy(i).wait_recv()
 
-    out[...] = rbuf[...].reshape(GROUP * COLS, BLK)
+    out[...] = rbuf[...].reshape(GROUP * COLS, BLK).T
 
     @pl.loop(0, GROUP - 1)
     def _(i):
@@ -341,9 +398,9 @@
     smem = pl.BlockSpec(memory_space=pltpu.SMEM)
     dma = pltpu.SemaphoreType.DMA
     bf16 = jnp.bfloat16
-    transposed = pl.pallas_call(
+    return pl.pallas_call(
         kernel,
-        out_shape=jax.ShapeDtypeStruct((GROUP * COLS, BLK), bf16),
+        out_shape=jax.ShapeDtypeStruct((BLK, GROUP * COLS), bf16),
         in_specs=[hbm, hbm, hbm, hbm, smem, hbm],
         out_specs=vmem,
         scratch_shapes=[
@@ -359,6 +416,7 @@
             pltpu.VMEM((GROUP, COLS, BLK), bf16),
             pltpu.VMEM((NX, 128), jnp.float32),
             pltpu.VMEM((1, SLOTS), jnp.int32),
+            dma((2, NX * NY - 1)),
             dma((2, NX * NY - 1)),
             dma((2, NX * NY - 1)),
             dma((2, GROUP - 1)),
@@ -377,7 +435,6 @@
             collective_id=0, has_side_effects=True, vmem_limit_bytes=56 * 2**20
         ),
     )(features.T, weight, bias.reshape(NX, 128), tile_src, tile_count, tile_vals)
-    return transposed.T
 
 
 def solution(mesh):

time: 94.7 us -> 90.4 us (0.955)
  Pallas kernels: 92.3 us -> 88.1 us
    pallas_call x1, Pallas kernels: 92.3 us -> 88.1 us  [shards(): pl.pallas_call(kernel, out_shape=jax.ShapeDtypeStruct((BLK, GROUP * COLS)...]
    transpose x1 -> x0, local copies, waits for them, and re-layouts: 1.67 us -> none  [shards(): return transposed.T]
    unnamed x0 -> x1, local copies, waits for them, and re-layouts: none -> 1.57 us
where the time goes in v4:
time: 90.4 us; the launch traced here: 90.3 us
  Pallas kernels  88.1 us (97%)
  local copies, waits for them, and re-layouts  1.57 us (2%)
    pallas_call x1, Pallas kernels, shards(): pl.pallas_call(kernel, out_shape=jax.ShapeDtypeStruct((BLK, GROUP * COLS)...  88.1 us

profile of v4, /device:TPU:1, one launch (start us, length us, event | category | flops | bytes accessed | tf_op | source)
XLA Modules:
  0.0 90.3 jit_solution(13206120619758841172)
XLA Ops:
  0.7 88.1 %shard_map.64 = bf16[128,512]{1,0:T(8,128)(2,1)} custom-call(bf16[48,2048]{1,0:T(8,128)(2,1)} %bitcast.2, bf16[48,512]{1,0:T(8,128)(2,1)} %w.1, f32[4,128]{1,0:T(4,128)} %bitcast.3, s32[1,32]{1,0:T(1,128)} %src.1, s32[1]{0:T(128)S(6)} %copy.8.cnt, bf16[1,32,128,128]{3,2,1,0:T(8,128)(2,1)} %tiles.1), custom_call_target="tpu_custom_call" | custom-call | tf_op jit(solution)/shard_map/pallas_call | solution.py:401
  88.7 1.6 %copy.9 = bf16[128,512]{1,0:T(8,128)(2,1)} copy(bf16[128,512]{1,0:T(8,128)(2,1)} %shard_map.64) | data formatting | bytes 262144

commit v5 on v4

--- a/solution.py
+++ b/solution.py
@@ -15,13 +15,14 @@
 HALF = 3
 BLOCKS = NZ * NY * SHARD
 SLOTS = 32
-UNROLL = 8
+UNROLL = 32
 ROWS = 512
+DEPTH = 768
 ORDER = (
-    "R0 R1 P1 R2", "Y0 R3 R4 P2", "R5 Y1 R6 R7", "P3 R8 Y2 R9",
-    "R10 P4 R11 R12", "Y3 R13 P5 T0", "R14 R15 Y4 R16", "P6 R17 R18 Y5",
-    "R19 P7 T1 R20", "R21 R22 P8 R23", "R24 Y6 R25 R26", "T2 Y7 R27 Y8",
-    "R28 R30 R29 R31",
+    "R1 R2 R3 P1", "R4 Y0 R5 R6", "P2 R7 Y1 R8", "R9 P3 R10 Y2",
+    "R11 R12 P4 R13", "R14 Y3 R15 P5", "T0 R16 R17 Y4", "R18 P6 R19 R20",
+    "Y5 R21 P7 T1", "R22 R23 R24 P8", "R25 R26 Y6 R27", "T2 R28 R30 Y7",
+    "R29 R31 Y8",
 )
 PLANE = (
     (2, 2), (2, 1), (1, 2), (2, 3), (3, 2), (1, 1), (3, 3), (1, 3), (3, 1), (2, 0), (0, 2), (1, 0), (3, 0), (0, 1), (0, 3),
@@ -31,7 +32,7 @@
 def kernel(
     ft, w, bias, src, cnt, tiles, out,
     xbuf, wbuf, hb, stage, tbuf, sv, ss, bt, obuf, rbuf,
-    bv, iv, x_sem, w_sem, v_sem, s_sem, ss_sem, t_sem, local_sem, h_sem, ry_sem, pz_sem, rz_sem, py_sem, pf_sem, o_sem,
+    bv, iv, wt, x_sem, w_sem, v_sem, s_sem, ss_sem, t_sem, local_sem, h_sem, ry_sem, pz_sem, rz_sem, py_sem, pf_sem, o_sem,
 ):
     n = lax.axis_index("node")
     f = lax.axis_index("feat")
@@ -79,14 +80,18 @@
     for device in (sibling, above, below):
         pl.semaphore_signal(barrier, inc=1, device_id=device, device_id_type=MESH)
 
+    def x_rows(yy, phase):
+        return pl.ds(pl.multiple_of(yy * ROWS + (1 - phase) * (ROWS // 2), ROWS // 2), ROWS // 2)
+
     local = [
         pltpu.make_async_copy(source, target, local_sem.at[i])
         for i, (source, target) in enumerate((
             (tiles.at[0], tbuf.at[me]),
             (bias, bv),
             (src, iv),
-            (ft.at[:, pl.ds(pl.multiple_of(y * ROWS, ROWS), ROWS)], xbuf.at[f]),
-            (w.at[:, pl.ds(pl.multiple_of(x * 128, 128), 128)], wbuf.at[f]),
+            (ft.at[:, x_rows(y, 0)], xbuf.at[0, len(PLANE)]),
+            (ft.at[:, x_rows(y, 1)], xbuf.at[1, len(PLANE)]),
+            (w.at[:, pl.ds(pl.multiple_of(x * 128, 128), 128)], wbuf.at[len(PLANE)]),
         ))
     ]
     for copy in local:
@@ -98,15 +103,16 @@
         dx, dy = PLANE[i]
         return up(x, NX, dx), up(y, NY, dy)
 
-    def x_copy(i):
+    def x_copy(i, phase):
         xx, yy = plane_peer(i)
-        rows = pl.ds(pl.multiple_of(yy * ROWS, ROWS), ROWS)
-        return remote(ft.at[:, rows], xbuf.at[f], x_sem, (i,), at(xx, yy, z, c))
+        return remote(
+            ft.at[:, x_rows(yy, phase)], xbuf.at[phase, i], x_sem, (phase, i), at(xx, yy, z, c)
+        )
 
     def w_copy(i):
         xx, yy = plane_peer(i)
         columns = pl.ds(pl.multiple_of(xx * 128, 128), 128)
-        return remote(w.at[:, columns], wbuf.at[f], w_sem, (i,), at(xx, yy, z, c))
+        return remote(w.at[:, columns], wbuf.at[i], w_sem, (i,), at(xx, yy, z, c))
 
     def w_shares(method):
         for core in range(2):
@@ -117,8 +123,8 @@
                     method(i)
 
     w_shares(lambda i: w_copy(i).start())
-    x_plane = [x_copy(i) for i in range(len(PLANE))]
-    for copy in x_plane:
+    x_plane = [[x_copy(i, phase) for i in range(len(PLANE))] for phase in range(2)]
+    for copy in x_plane[0] + x_plane[1]:
         copy.start()
 
     hb[BLOCKS] = jnp.zeros((COLS, BLK), jnp.bfloat16)
@@ -128,7 +134,7 @@
     s = iv[...]
     zz, rest = lax.shift_right_logical(s, 5), s & 31
     cc, ff = lax.shift_right_logical(rest, 4), rest & 15
-    place = (zz * NY + lax.shift_right_logical(ff, 2)) * SHARD + cc * 4 + (ff & 3)
+    place = (zz * NY + lax.shift_right_logical(ff, 2)) * SHARD + (ff & 2) * 2 + cc * 2 + (ff & 1)
     alive = lax.broadcasted_iota(jnp.int32, s.shape, 1) < cnt[0]
     sv[me] = jnp.zeros((8, 128), jnp.int32)
     sv[me, 0:1, 0:SLOTS] = jnp.where(alive, place, BLOCKS)
@@ -139,20 +145,15 @@
 
     for i in range(GROUP - 1):
         s_copy(i).start()
-    local[3].wait()
-    local[4].wait()
+    local[5].wait()
     def hand_on(i):
-        dx, dy = PLANE[i]
-        ref = wbuf.at[down(x, NX, dx) * NY + down(y, NY, dy)]
-        return remote(ref, ref, v_sem, (i,), sibling)
+        return remote(wbuf.at[i], wbuf.at[i], v_sem, (i,), sibling)
 
     def pass_weights(i):
         w_copy(i).wait_recv()
         hand_on(i).start()
 
     w_shares(pass_weights)
-    for copy in x_plane:
-        copy.wait_recv()
     for core in range(2):
 
         @pl.when(c == core)
@@ -160,44 +161,34 @@
             for i in range(1 - core, len(PLANE), 2):
                 hand_on(i).wait_recv()
 
-
-    own = tiles.at[0]
-    low, high = pl.ds(0, SLOTS // 2), pl.ds(SLOTS // 2, SLOTS // 2)
-    t_low_right = remote(own.at[low], tbuf.at[me, low], t_sem, (0,), right)
-    t_high_left = remote(own.at[high], tbuf.at[me, high], t_sem, (1,), left)
-    t_high_right = remote(own.at[high], tbuf.at[me, high], t_sem, (2,), right)
-    t_low_left = remote(own.at[low], tbuf.at[me, low], t_sem, (3,), left)
-    t_own_sibling = remote(own, tbuf.at[me], t_sem, (4,), sibling)
-    for copy in (t_low_right, t_high_left, t_high_right, t_low_left):
-        copy.start()
-    from_left, from_right, from_far = (down(x, NX) * 2 + c, up(x, NX) * 2 + c, up(x, NX, 2) * 2 + c)
-    t_pass_right = remote(tbuf.at[from_left, low], tbuf.at[from_left, low], t_sem, (5,), right)
-    t_pass_left = remote(tbuf.at[from_right, high], tbuf.at[from_right, high], t_sem, (6,), left)
-    t_sibling = [
-        remote(tbuf.at[e], tbuf.at[e], t_sem, (7 + j,), sibling)
-        for j, e in enumerate((from_left, from_right, from_far))
-    ]
-
-    t_from_right = remote(tbuf.at[from_far, low], tbuf.at[from_far, low], t_sem, (5,), right)
-    t_from_left = remote(tbuf.at[from_far, high], tbuf.at[from_far, high], t_sem, (6,), left)
-    places = pltpu.make_async_copy(sv, ss, ss_sem.at[0])
-
-    ht = lax.dot_general(
-        wbuf[...].reshape(NX * NY * 48, 128), xbuf[...].reshape(NX * NY * 48, 512),
-        (((0,), (0,)), ((), ())), preferred_element_type=jnp.float32,
-    ).astype(jnp.bfloat16)
-    mine = jnp.where(c == 0, ht[:COLS], ht[COLS:])
-    other = jnp.where(c == 0, ht[COLS:], ht[:COLS])
-    place_of = lambda zz, yy: (zz * NY + yy) * SHARD
-    base = place_of(z, y) + c * 4
-    for k in range(4):
-        stage[k] = other[:, k * BLK : (k + 1) * BLK]
-    h_copy = remote(stage, hb.at[pl.ds(base, 4)], h_sem, (0,), sibling)
-    h_copy.start()
-    t_own_sibling.start()
-    for k in range(4):
-        hb[base + k] = mine[:, k * BLK : (k + 1) * BLK]
-    h_copy.wait_recv()
+    wt[...] = wbuf[...].reshape(DEPTH, 128).T
+
+    def transform(core, phase):
+        columns = wt[pl.ds(pl.multiple_of(core * COLS, COLS), COLS), :]
+        hidden = jnp.dot(columns, xbuf[phase].reshape(DEPTH, ROWS // 2), preferred_element_type=jnp.float32)
+        return hidden.astype(jnp.bfloat16)
+
+    def place_of(zz, yy):
+        return (zz * NY + yy) * SHARD
+
+    def h_copy(phase):
+        base = place_of(z, y) + 4 * (1 - phase) + 2 * c
+        return remote(stage.at[pl.ds(2 * phase, 2)], hb.at[pl.ds(base, 2)], h_sem, (phase,), sibling)
+
+    def make_hidden(phase):
+        other = transform(1 - c, phase)
+        for k in range(2):
+            stage[2 * phase + k] = other[:, k * BLK : (k + 1) * BLK]
+        h_copy(phase).start()
+        mine = transform(c, phase)
+        for k in range(2):
+            hb[place_of(z, y) + 4 * (1 - phase) + 2 * c + k] = mine[:, k * BLK : (k + 1) * BLK]
+
+    local[3].wait()
+    for copy in x_plane[0]:
+        copy.wait_recv()
+    make_hidden(0)
+    h_copy(0).wait_recv()
 
     def blocks(zz, yy, first, count):
         return hb.at[pl.ds(place_of(zz, yy) + first, count)]
@@ -316,6 +307,34 @@
 
     for j in range(1, NY):
         ry_copy(j).start()
+    r_step(0)
+
+    own = tiles.at[0]
+    low, high = pl.ds(0, SLOTS // 2), pl.ds(SLOTS // 2, SLOTS // 2)
+    t_low_right = remote(own.at[low], tbuf.at[me, low], t_sem, (0,), right)
+    t_high_left = remote(own.at[high], tbuf.at[me, high], t_sem, (1,), left)
+    t_high_right = remote(own.at[high], tbuf.at[me, high], t_sem, (2,), right)
+    t_low_left = remote(own.at[low], tbuf.at[me, low], t_sem, (3,), left)
+    t_own_sibling = remote(own, tbuf.at[me], t_sem, (4,), sibling)
+    from_left, from_right, from_far = (down(x, NX) * 2 + c, up(x, NX) * 2 + c, up(x, NX, 2) * 2 + c)
+    t_pass_right = remote(tbuf.at[from_left, low], tbuf.at[from_left, low], t_sem, (5,), right)
+    t_pass_left = remote(tbuf.at[from_right, high], tbuf.at[from_right, high], t_sem, (6,), left)
+    t_sibling = [
+        remote(tbuf.at[e], tbuf.at[e], t_sem, (7 + j,), sibling)
+        for j, e in enumerate((from_left, from_right, from_far))
+    ]
+
+    t_from_right = remote(tbuf.at[from_far, low], tbuf.at[from_far, low], t_sem, (5,), right)
+    t_from_left = remote(tbuf.at[from_far, high], tbuf.at[from_far, high], t_sem, (6,), left)
+    places = pltpu.make_async_copy(sv, ss, ss_sem.at[0])
+
+    local[4].wait()
+    for copy in x_plane[1]:
+        copy.wait_recv()
+    make_hidden(1)
+    for copy in (t_low_right, t_high_left, t_high_right, t_low_left, t_own_sibling):
+        copy.start()
+    h_copy(1).wait_recv()
     for copy in p_copies(0):
         copy.start()
     spread(0)
@@ -356,7 +375,7 @@
 
     rbuf[me] = aggregate(me)
 
-    for copy in x_plane:
+    for copy in x_plane[0] + x_plane[1]:
         copy.wait_send()
 
     def w_over(i):
@@ -367,7 +386,7 @@
 
     for i in range(GROUP - 1):
         s_copy(i).wait_send()
-    for copy in (t_low_right, t_high_left, t_high_right, t_low_left, t_own_sibling, t_pass_right, t_pass_left, h_copy):
+    for copy in (t_low_right, t_high_left, t_high_right, t_low_left, t_own_sibling, t_pass_right, t_pass_left, h_copy(0), h_copy(1)):
         copy.wait_send()
     for copy in t_sibling:
         copy.wait_send()
@@ -404,7 +423,7 @@
         in_specs=[hbm, hbm, hbm, hbm, smem, hbm],
         out_specs=vmem,
         scratch_shapes=[
-            pltpu.VMEM((NX * NY, depth, rows // NY), bf16),
+            pltpu.VMEM((2, NX * NY, depth, ROWS // 2), bf16),
             pltpu.VMEM((NX * NY, depth, 128), bf16),
             pltpu.VMEM((BLOCKS + 1, COLS, BLK), bf16),
             pltpu.VMEM((4, COLS, BLK), bf16),
@@ -416,14 +435,15 @@
             pltpu.VMEM((GROUP, COLS, BLK), bf16),
             pltpu.VMEM((NX, 128), jnp.float32),
             pltpu.VMEM((1, SLOTS), jnp.int32),
-            dma((2, NX * NY - 1)),
+            pltpu.VMEM((128, DEPTH), bf16),
+            dma((2, 2, NX * NY - 1)),
             dma((2, NX * NY - 1)),
             dma((2, NX * NY - 1)),
             dma((2, GROUP - 1)),
             dma((1,)),
             dma((2, 10)),
-            dma((5,)),
-            dma((2, 1)),
+            dma((6,)),
+            dma((2, 2)),
             dma((2, NY - 1)),
             dma((2, 2, NZ // 2)),
             dma((2, 2, NY, NZ // 2)),

time: 90.4 us -> 89.7 us (level)
  no operation moved by 1% of the time
where the time goes in v5:
time: 89.7 us; the launch traced here: 89.6 us
  Pallas kernels  87.4 us (97%)
  local copies, waits for them, and re-layouts  1.57 us (2%)
    pallas_call x1, Pallas kernels, shards(): pl.pallas_call(kernel, out_shape=jax.ShapeDtypeStruct((BLK, GROUP * COLS)...  87.4 us

profile of v5, /device:TPU:1, one launch (start us, length us, event | category | flops | bytes accessed | tf_op | source)
XLA Modules:
  0.0 89.6 jit_solution(4216360822719859930)
XLA Ops:
  0.7 87.4 %shard_map.64 = bf16[128,512]{1,0:T(8,128)(2,1)} custom-call(bf16[48,2048]{1,0:T(8,128)(2,1)} %bitcast.2, bf16[48,512]{1,0:T(8,128)(2,1)} %w.1, f32[4,128]{1,0:T(4,128)} %bitcast.3, s32[1,32]{1,0:T(1,128)} %src.1, s32[1]{0:T(128)S(6)} %copy.8.cnt, bf16[1,32,128,128]{3,2,1,0:T(8,128)(2,1)} %tiles.1), custom_call_target="tpu_custom_call" | custom-call | tf_op jit(solution)/shard_map/pallas_call | solution.py:420
  88.0 1.6 %copy.9 = bf16[128,512]{1,0:T(8,128)(2,1)} copy(bf16[128,512]{1,0:T(8,128)(2,1)} %shard_map.64) | data formatting | bytes 262144

commit v6 on v4

--- a/solution.py
+++ b/solution.py
@@ -15,8 +15,10 @@
 HALF = 3
 BLOCKS = NZ * NY * SHARD
 SLOTS = 32
-UNROLL = 8
+UNROLL = 32
 ROWS = 512
+DEPTH = 768
+DIRECT, RELAYED = 11, 4
 ORDER = (
     "R0 R1 P1 R2", "Y0 R3 R4 P2", "R5 Y1 R6 R7", "P3 R8 Y2 R9",
     "R10 P4 R11 R12", "Y3 R13 P5 T0", "R14 R15 Y4 R16", "P6 R17 R18 Y5",
@@ -24,14 +26,14 @@
     "R28 R30 R29 R31",
 )
 PLANE = (
-    (2, 2), (2, 1), (1, 2), (2, 3), (3, 2), (1, 1), (3, 3), (1, 3), (3, 1), (2, 0), (0, 2), (1, 0), (3, 0), (0, 1), (0, 3),
+    (1, 0), (3, 1), (1, 2), (3, 3), (1, 1), (3, 0), (1, 3), (3, 2), (0, 1), (0, 3), (0, 2), (2, 0), (2, 1), (2, 2), (2, 3),
 )
 
 
 def kernel(
     ft, w, bias, src, cnt, tiles, out,
     xbuf, wbuf, hb, stage, tbuf, sv, ss, bt, obuf, rbuf,
-    bv, iv, x_sem, w_sem, v_sem, s_sem, ss_sem, t_sem, local_sem, h_sem, ry_sem, pz_sem, rz_sem, py_sem, pf_sem, o_sem,
+    bv, iv, wt, ht, r_sem, x_sem, w_sem, v_sem, s_sem, ss_sem, t_sem, local_sem, h_sem, ry_sem, pz_sem, rz_sem, py_sem, pf_sem, o_sem,
 ):
     n = lax.axis_index("node")
     f = lax.axis_index("feat")
@@ -85,8 +87,8 @@
             (tiles.at[0], tbuf.at[me]),
             (bias, bv),
             (src, iv),
-            (ft.at[:, pl.ds(pl.multiple_of(y * ROWS, ROWS), ROWS)], xbuf.at[f]),
-            (w.at[:, pl.ds(pl.multiple_of(x * 128, 128), 128)], wbuf.at[f]),
+            (ft.at[:, pl.ds(pl.multiple_of(y * ROWS, ROWS), ROWS)], xbuf.at[len(PLANE)]),
+            (w.at[:, pl.ds(pl.multiple_of(x * 128, 128), 128)], wbuf.at[len(PLANE)]),
         ))
     ]
     for copy in local:
@@ -101,12 +103,12 @@
     def x_copy(i):
         xx, yy = plane_peer(i)
         rows = pl.ds(pl.multiple_of(yy * ROWS, ROWS), ROWS)
-        return remote(ft.at[:, rows], xbuf.at[f], x_sem, (i,), at(xx, yy, z, c))
+        return remote(ft.at[:, rows], xbuf.at[i], x_sem, (i,), at(xx, yy, z, c))
 
     def w_copy(i):
         xx, yy = plane_peer(i)
         columns = pl.ds(pl.multiple_of(xx * 128, 128), 128)
-        return remote(w.at[:, columns], wbuf.at[f], w_sem, (i,), at(xx, yy, z, c))
+        return remote(w.at[:, columns], wbuf.at[i], w_sem, (i,), at(xx, yy, z, c))
 
     def w_shares(method):
         for core in range(2):
@@ -116,10 +118,15 @@
                 for i in range(core, len(PLANE), 2):
                     method(i)
 
+    x_plane = [x_copy(i) for i in range(DIRECT)]
+    for copy in x_plane[:RELAYED]:
+        copy.start()
     w_shares(lambda i: w_copy(i).start())
-    x_plane = [x_copy(i) for i in range(len(PLANE))]
-    for copy in x_plane:
-        copy.start()
+    for copy in x_plane[RELAYED:]:
+        copy.start()
+
+    def relay(i):
+        return remote(xbuf.at[i], xbuf.at[DIRECT + i], r_sem, (i,), (right, left)[i % 2])
 
     hb[BLOCKS] = jnp.zeros((COLS, BLK), jnp.bfloat16)
     local[1].wait()
@@ -139,20 +146,19 @@
 
     for i in range(GROUP - 1):
         s_copy(i).start()
-    local[3].wait()
     local[4].wait()
     def hand_on(i):
-        dx, dy = PLANE[i]
-        ref = wbuf.at[down(x, NX, dx) * NY + down(y, NY, dy)]
-        return remote(ref, ref, v_sem, (i,), sibling)
+        return remote(wbuf.at[i], wbuf.at[i], v_sem, (i,), sibling)
 
     def pass_weights(i):
         w_copy(i).wait_recv()
         hand_on(i).start()
 
     w_shares(pass_weights)
-    for copy in x_plane:
-        copy.wait_recv()
+    relays = [relay(i) for i in range(RELAYED)]
+    for arrival, copy in zip(x_plane, relays):
+        arrival.wait_recv()
+        copy.start()
     for core in range(2):
 
         @pl.when(c == core)
@@ -160,6 +166,21 @@
             for i in range(1 - core, len(PLANE), 2):
                 hand_on(i).wait_recv()
 
+    wt[...] = wbuf[...].reshape(DEPTH, 128).T
+    half = DEPTH // 2
+
+    def transform(core, part):
+        columns = wt[pl.ds(pl.multiple_of(core * COLS, COLS), COLS), part * half : (part + 1) * half]
+        rows = xbuf[part * 8 : (part + 1) * 8].reshape(half, ROWS)
+        return jnp.dot(columns, rows, preferred_element_type=jnp.float32)
+
+    for copy in x_plane[RELAYED:8]:
+        copy.wait_recv()
+    for core in range(2):
+        ht[core] = transform(core, 0)
+    local[3].wait()
+    for copy in x_plane[8:] + relays:
+        copy.wait_recv()
 
     own = tiles.at[0]
     low, high = pl.ds(0, SLOTS // 2), pl.ds(SLOTS // 2, SLOTS // 2)
@@ -182,19 +203,15 @@
     t_from_left = remote(tbuf.at[from_far, high], tbuf.at[from_far, high], t_sem, (6,), left)
     places = pltpu.make_async_copy(sv, ss, ss_sem.at[0])
 
-    ht = lax.dot_general(
-        wbuf[...].reshape(NX * NY * 48, 128), xbuf[...].reshape(NX * NY * 48, 512),
-        (((0,), (0,)), ((), ())), preferred_element_type=jnp.float32,
-    ).astype(jnp.bfloat16)
-    mine = jnp.where(c == 0, ht[:COLS], ht[COLS:])
-    other = jnp.where(c == 0, ht[COLS:], ht[:COLS])
     place_of = lambda zz, yy: (zz * NY + yy) * SHARD
     base = place_of(z, y) + c * 4
+    other = (ht[1 - c] + transform(1 - c, 1)).astype(jnp.bfloat16)
     for k in range(4):
         stage[k] = other[:, k * BLK : (k + 1) * BLK]
     h_copy = remote(stage, hb.at[pl.ds(base, 4)], h_sem, (0,), sibling)
     h_copy.start()
     t_own_sibling.start()
+    mine = (ht[c] + transform(c, 1)).astype(jnp.bfloat16)
     for k in range(4):
         hb[base + k] = mine[:, k * BLK : (k + 1) * BLK]
     h_copy.wait_recv()
@@ -356,7 +373,7 @@
 
     rbuf[me] = aggregate(me)
 
-    for copy in x_plane:
+    for copy in x_plane + relays:
         copy.wait_send()
 
     def w_over(i):
@@ -416,6 +433,9 @@
             pltpu.VMEM((GROUP, COLS, BLK), bf16),
             pltpu.VMEM((NX, 128), jnp.float32),
             pltpu.VMEM((1, SLOTS), jnp.int32),
+            pltpu.VMEM((128, DEPTH), bf16),
+            pltpu.VMEM((2, COLS, ROWS), jnp.float32),
+            dma((2, RELAYED)),
             dma((2, NX * NY - 1)),
             dma((2, NX * NY - 1)),
             dma((2, NX * NY - 1)),

time: 90.4 us -> 89.2 us (0.987)
  Pallas kernels: 88.1 us -> 86.9 us
    pallas_call x1, Pallas kernels: 88.1 us -> 86.9 us  [shards(): pl.pallas_call(kernel, out_shape=jax.ShapeDtypeStruct((BLK, GROUP * COLS)...]
where the time goes in v6:
time: 89.2 us; the launch traced here: 89.1 us
  Pallas kernels  86.9 us (97%)
  local copies, waits for them, and re-layouts  1.57 us (2%)
    pallas_call x1, Pallas kernels, shards(): pl.pallas_call(kernel, out_shape=jax.ShapeDtypeStruct((BLK, GROUP * COLS)...  86.9 us

profile of v6, /device:TPU:1, one launch (start us, length us, event | category | flops | bytes accessed | tf_op | source)
XLA Modules:
  0.0 89.1 jit_solution(15410444911199242808)
XLA Ops:
  0.7 86.9 %shard_map.64 = bf16[128,512]{1,0:T(8,128)(2,1)} custom-call(bf16[48,2048]{1,0:T(8,128)(2,1)} %bitcast.2, bf16[48,512]{1,0:T(8,128)(2,1)} %w.1, f32[4,128]{1,0:T(4,128)} %bitcast.3, s32[1,32]{1,0:T(1,128)} %src.1, s32[1]{0:T(128)S(6)} %copy.8.cnt, bf16[1,32,128,128]{3,2,1,0:T(8,128)(2,1)} %tiles.1), custom_call_target="tpu_custom_call" | custom-call | tf_op jit(solution)/shard_map/pallas_call | solution.py:418
  87.5 1.6 %copy.9 = bf16[128,512]{1,0:T(8,128)(2,1)} copy(bf16[128,512]{1,0:T(8,128)(2,1)} %shard_map.64) | data formatting | bytes 262144

commit v7 on v6

--- a/solution.py
+++ b/solution.py
@@ -61,13 +61,17 @@
     front, back = at(x, up(y, NY), z, c), at(x, down(y, NY), z, c)
     above, below = at(x, y, up(z, NZ), c), at(x, y, down(z, NZ), c)
 
+    def group_offset(i):
+        k = lax.div(i, 2)
+        return lax.rem(2 + 3 * k + 3 * lax.div(k * (k - 1), 2), NX), 1 - lax.rem(i, 2)
+
     def group_peer(i):
-        dx, dc = lax.rem(1 + lax.div(i, 2), NX), 1 - lax.rem(i, 2)
+        dx, dc = group_offset(i)
         xx, cc = up(x, NX, dx), lax.rem(c + dc, 2)
         return xx * 2 + cc, at(xx, y, z, cc)
 
     def group_source(i):
-        dx, dc = lax.rem(1 + lax.div(i, 2), NX), 1 - lax.rem(i, 2)
+        dx, dc = group_offset(i)
         return down(x, NX, dx) * 2 + lax.rem(c + dc, 2)
 
     barrier = pltpu.get_barrier_semaphore()
@@ -128,6 +132,23 @@
     def relay(i):
         return remote(xbuf.at[i], xbuf.at[DIRECT + i], r_sem, (i,), (right, left)[i % 2])
 
+    def s_copy(i):
+        _, device = group_peer(i)
+        return remote(sv.at[me], sv.at[me], s_sem, (i,), device)
+
+    local[4].wait()
+    def hand_on(i):
+        return remote(wbuf.at[i], wbuf.at[i], v_sem, (i,), sibling)
+
+    def pass_weights(i):
+        w_copy(i).wait_recv()
+        hand_on(i).start()
+
+    relays = [relay(i) for i in range(RELAYED)]
+    for arrival, copy in zip(x_plane, relays):
+        arrival.wait_recv()
+        copy.start()
+    w_shares(pass_weights)
     hb[BLOCKS] = jnp.zeros((COLS, BLK), jnp.bfloat16)
     local[1].wait()
     bt[...] = jnp.broadcast_to(bv[pl.ds(x, 1), :], (128, 128)).T
@@ -140,25 +161,8 @@
     sv[me] = jnp.zeros((8, 128), jnp.int32)
     sv[me, 0:1, 0:SLOTS] = jnp.where(alive, place, BLOCKS)
 
-    def s_copy(i):
-        _, device = group_peer(i)
-        return remote(sv.at[me], sv.at[me], s_sem, (i,), device)
-
     for i in range(GROUP - 1):
         s_copy(i).start()
-    local[4].wait()
-    def hand_on(i):
-        return remote(wbuf.at[i], wbuf.at[i], v_sem, (i,), sibling)
-
-    def pass_weights(i):
-        w_copy(i).wait_recv()
-        hand_on(i).start()
-
-    w_shares(pass_weights)
-    relays = [relay(i) for i in range(RELAYED)]
-    for arrival, copy in zip(x_plane, relays):
-        arrival.wait_recv()
-        copy.start()
     for core in range(2):
 
         @pl.when(c == core)

time: 89.2 us -> 87.7 us (0.983)
  Pallas kernels: 86.9 us -> 85.4 us
    pallas_call x1, Pallas kernels: 86.9 us -> 85.4 us  [shards(): pl.pallas_call(kernel, out_shape=jax.ShapeDtypeStruct((BLK, GROUP * COLS)...]
where the time goes in v7:
time: 87.7 us; the launch traced here: 87.6 us
  Pallas kernels  85.4 us (97%)
  local copies, waits for them, and re-layouts  1.57 us (2%)
    pallas_call x1, Pallas kernels, shards(): pl.pallas_call(kernel, out_shape=jax.ShapeDtypeStruct((BLK, GROUP * COLS)...  85.4 us

profile of v7, /device:TPU:1, one launch (start us, length us, event | category | flops | bytes accessed | tf_op | source)
XLA Modules:
  0.0 87.6 jit_solution(4105759185158769834)
XLA Ops:
  0.7 85.4 %shard_map.64 = bf16[128,512]{1,0:T(8,128)(2,1)} custom-call(bf16[48,2048]{1,0:T(8,128)(2,1)} %bitcast.2, bf16[48,512]{1,0:T(8,128)(2,1)} %w.1, f32[4,128]{1,0:T(4,128)} %bitcast.3, s32[1,32]{1,0:T(1,128)} %src.1, s32[1]{0:T(128)S(6)} %copy.8.cnt, bf16[1,32,128,128]{3,2,1,0:T(8,128)(2,1)} %tiles.1), custom_call_target="tpu_custom_call" | custom-call | tf_op jit(solution)/shard_map/pallas_call | solution.py:422
  86.0 1.6 %copy.9 = bf16[128,512]{1,0:T(8,128)(2,1)} copy(bf16[128,512]{1,0:T(8,128)(2,1)} %shard_map.64) | data formatting | bytes 262144

commit v8 on v7

--- a/solution.py
+++ b/solution.py
@@ -26,7 +26,7 @@
     "R28 R30 R29 R31",
 )
 PLANE = (
-    (1, 0), (3, 1), (1, 2), (3, 3), (1, 1), (3, 0), (1, 3), (3, 2), (0, 1), (0, 3), (0, 2), (2, 0), (2, 1), (2, 2), (2, 3),
+    (1, 0), (3, 3), (1, 1), (3, 2), (1, 2), (3, 0), (1, 3), (3, 1), (0, 2), (0, 1), (0, 3), (2, 0), (2, 3), (2, 1), (2, 2),
 )
 
 

time: 87.7 us -> 87.6 us (level)
  no operation moved by 1% of the time
where the time goes in v8:
time: 87.6 us; the launch traced here: 87.4 us
  Pallas kernels  85.2 us (97%)
  local copies, waits for them, and re-layouts  1.57 us (2%)
    pallas_call x1, Pallas kernels, shards(): pl.pallas_call(kernel, out_shape=jax.ShapeDtypeStruct((BLK, GROUP * COLS)...  85.2 us

profile of v8, /device:TPU:1, one launch (start us, length us, event | category | flops | bytes accessed | tf_op | source)
XLA Modules:
  0.0 87.4 jit_solution(14265212896687324879)
XLA Ops:
  0.7 85.2 %shard_map.64 = bf16[128,512]{1,0:T(8,128)(2,1)} custom-call(bf16[48,2048]{1,0:T(8,128)(2,1)} %bitcast.2, bf16[48,512]{1,0:T(8,128)(2,1)} %w.1, f32[4,128]{1,0:T(4,128)} %bitcast.3, s32[1,32]{1,0:T(1,128)} %src.1, s32[1]{0:T(128)S(6)} %copy.8.cnt, bf16[1,32,128,128]{3,2,1,0:T(8,128)(2,1)} %tiles.1), custom_call_target="tpu_custom_call" | custom-call | tf_op jit(solution)/shard_map/pallas_call | solution.py:422
  85.9 1.6 %copy.9 = bf16[128,512]{1,0:T(8,128)(2,1)} copy(bf16[128,512]{1,0:T(8,128)(2,1)} %shard_map.64) | data formatting | bytes 262144
